TPU v7x, 128 devices: a whole 4x4x4 slice. The times are simulated.
128 devices in a mesh: view: 4 (over z), tile: 32 (over x, y, core).
Axes of the slice: x: 4, y: 4, z: 4, core: 2. Of those that a mesh axis runs over, the one named last changes fastest.
Arguments:
- centres: float32 [3, 131072], P(None, ('view', 'tile')), may hold values from -6 to 6
- shape_raw: float32 [6, 131072], P(None, ('view', 'tile')), may hold values from -1 to 0.2
- opacity_logit: float32 [131072], P(('view', 'tile')), may hold values from -6 to -1
- colours: float32 [3, 131072], P(None, ('view', 'tile')), may hold values from -6 to 6
- camera: float32 [8, 2, 4], replicated, may hold values from -15 to 15
- target: float32 [8, 512, 3, 256], P('view', 'tile'), may hold values from -3 to 3
- intersection_ids: int32 [8, 512, 256], P('view', 'tile'), may hold values from 0 to 131071, as said below
- depth_order: int32 [8, 512, 256], P('view', 'tile'), may hold values from 0 to 255, each once within a row
- live_count: int32 [8, 512], P('view', 'tile'), may hold values from 1 to 256, as said below
Outputs:
- rendered: float32 [8, 512, 3, 256], P('view', 'tile')
- grad_centres: float32 [3, 131072], P(None, ('view', 'tile'))
- grad_shape: float32 [6, 131072], P(None, ('view', 'tile'))
- grad_opacity: float32 [131072], P(('view', 'tile'))
- grad_colours: float32 [3, 131072], P(None, ('view', 'tile'))
- next_owner: int32 [8, 512], P('view', 'tile')
Inputs may be any that keep to these rules, and one draw needn't show every extreme that they name: `intersection_ids`: gaussian g is held by device g div 1024, devices counted along view+tile. Among the 2 x 16 x 256 slots held by one device at most 128 name Gaussians of any one device, and in every draw some device is named exactly 128 times by the slots of every device. `depth_order`: each tile's entries are a permutation of the slot numbers. Slot s of tile (v, t) is live when s < live_count[v, t]; every view has a tile with all 256 slots live.
All inputs are finite; a program needn't handle non-finite values.
Results may differ from a plain program's by a relative error of at most 0.0003.
Values sent between devices are 32-bit elements; how exact they have to be, the bound alone decides.
A program may use at most 128 MiB of HBM per device.

v0:
```python
from functools import partial
import math

import jax
import jax.numpy as jnp
from jax import lax
from jax.sharding import PartitionSpec as P

SIDE = 16


exact_mode = lax.Precision.HIGHEST


def prefix(array, axis, combine, identity):
    length, place = (lax.axis_size(axis), lax.axis_index(axis))
    everything = lax.all_gather(array, axis)
    start = jnp.broadcast_to(jnp.asarray(identity, array.dtype), array.shape)

    def step(k, before):
        reached = k < place
        new = combine(before, everything[k])
        return jnp.where(reached, new, before)

    return lax.fori_loop(0, length, step, start)


def lower_factor(shape_raw):
    empty_cells = jnp.zeros_like(shape_raw[0])
    first_row = jnp.stack([jnp.exp(shape_raw[0]), empty_cells, empty_cells])
    second_row = jnp.stack([shape_raw[1], jnp.exp(shape_raw[2]), empty_cells])
    third_row = jnp.stack([shape_raw[3], shape_raw[4], jnp.exp(shape_raw[5])])
    return jnp.stack([first_row, second_row, third_row])


def project(centres, shape_raw, opacity_logit, colours, camera):
    view_count = camera.shape[0]
    gaussians = centres.shape[1]
    linear = camera[:, :, 0:3]
    screen = (
        jnp.einsum("vij,jg->vig", linear, centres, precision=exact_mode)
        + camera[:, :, 3][:, :, None]
    )
    factor = jnp.einsum("vik,kjg->vijg", linear, lower_factor(shape_raw), precision=exact_mode)
    var_x = jnp.sum(factor[:, 0] * factor[:, 0], axis=1) + 0.3
    cov_xy = jnp.sum(factor[:, 0] * factor[:, 1], axis=1)
    var_y = jnp.sum(factor[:, 1] * factor[:, 1], axis=1) + 0.3
    determinant = var_x * var_y - cov_xy * cov_xy
    opacity = 0.95 / (1.0 + jnp.exp(-opacity_logit))
    fields = [
        screen[:, 0],
        screen[:, 1],
        var_y / determinant,
        -cov_xy / determinant,
        var_x / determinant,
        jnp.broadcast_to(opacity, (view_count, gaussians)),
    ]
    for channel in range(3):
        fields.append(jnp.broadcast_to(colours[channel], (view_count, gaussians)))
    return jnp.stack(fields)


def pixel_offsets():
    pixel_index = jnp.arange(SIDE * SIDE, dtype=jnp.int32)
    across = (pixel_index % SIDE).astype(jnp.float32) - (SIDE - 1) / 2.0
    downward = (pixel_index // SIDE).astype(jnp.float32) - (SIDE - 1) / 2.0
    return (across, downward)


def render_tile(slot_rec, order, live_count):
    slot_count = order.shape[0]
    picker = (
        order[:, None] == lax.broadcasted_iota(jnp.int32, (slot_count, slot_count), 1)
    ).astype(jnp.float32)
    ordered = jnp.einsum("ks,js->kj", slot_rec, picker, precision=exact_mode)
    active_slots = (order < live_count).astype(jnp.float32)
    across, downward = pixel_offsets()
    delta_x = across[:, None] - ordered[0][None, :]
    delta_y = downward[:, None] - ordered[1][None, :]
    radius = (
        ordered[2] * delta_x * delta_x
        + 2.0 * ordered[3] * delta_x * delta_y
        + ordered[4] * delta_y * delta_y
    )
    coverage = active_slots * ordered[5] * jnp.exp(-0.5 * radius)
    keep_log = jnp.log1p(-coverage)
    earlier = (
        lax.broadcasted_iota(jnp.int32, (slot_count, slot_count), 0)
        < lax.broadcasted_iota(jnp.int32, (slot_count, slot_count), 1)
    ).astype(jnp.float32)
    through = jnp.exp(jnp.dot(keep_log, earlier, precision=exact_mode))
    weights = through * coverage
    return jnp.einsum("ck,pk->cp", ordered[6:9], weights, precision=exact_mode)


def render_block(slot_rec, order, live_count):
    return jax.vmap(render_tile)(slot_rec, order, live_count)


def render_all(slot_rec, order, live_count):
    lead_count, tile_count, slot_count = order.shape
    total_tiles = lead_count * tile_count
    block_size = math.gcd(total_tiles, 8)
    records = jnp.moveaxis(slot_rec, 0, 2).reshape(
        total_tiles // block_size, block_size, 9, slot_count
    )
    orders = order.reshape(total_tiles // block_size, block_size, slot_count)
    counts = live_count.reshape(total_tiles // block_size, block_size)
    blocked = jax.checkpoint(render_block)

    def one_block(packed):
        return blocked(packed[0], packed[1], packed[2])

    images = lax.map(one_block, (records, orders, counts))
    return images.reshape(lead_count, tile_count, 3, SIDE * SIDE)


def add_counts(earlier, later):
    return earlier + later


def slot_ranks(owner_table):
    slots_here, devices = owner_table.shape
    block_rows = math.gcd(slots_here, 512)
    blocks = slots_here // block_rows
    grouped = owner_table.reshape(blocks, block_rows, devices)
    strict = (
        lax.broadcasted_iota(jnp.int32, (block_rows, block_rows), 1)
        < lax.broadcasted_iota(jnp.int32, (block_rows, block_rows), 0)
    ).astype(jnp.float32)
    inner = jnp.einsum("ij,njd->nid", strict, grouped, precision=exact_mode)
    block_totals = jnp.sum(grouped, axis=1)
    block_before = jnp.cumsum(block_totals, axis=0) - block_totals
    ranked = (inner + block_before[:, None, :]) * grouped
    return jnp.sum(ranked, axis=2).reshape(slots_here)


def fetch_rows(flat_rec, wanted):
    return jnp.take(flat_rec, wanted, axis=1)


def return_rows(values, wanted, columns):
    summed = jax.ops.segment_sum(jnp.transpose(values), wanted, num_segments=columns)
    return jnp.transpose(summed)


def shards(
    centres,
    shape_raw,
    opacity_logit,
    colours,
    camera,
    target,
    intersection_ids,
    depth_order,
    live_count,
):
    view_group = lax.axis_size("view")
    tile_group = lax.axis_size("tile")
    devices = view_group * tile_group
    own_count = centres.shape[1]
    views_here, tiles_here, slot_count = intersection_ids.shape
    slots_here = views_here * tiles_here * slot_count
    capacity = 2 * slots_here // devices
    totals = jnp.sum(live_count, axis=1)
    within = jnp.cumsum(live_count, axis=1) - live_count
    before = prefix(totals, "tile", add_counts, jnp.zeros_like(totals))
    whole = lax.psum(totals, "tile")
    before = before.astype(jnp.int32)
    next_owner = (before[:, None] + within) * tile_group // whole[:, None]
    project_here = partial(project, camera=camera)
    records, project_back = jax.vjp(project_here, centres, shape_raw, opacity_logit, colours)
    flat_rec = records.reshape(9, -1)
    rec_columns = flat_rec.shape[1]
    first_view = lax.axis_index("view") * views_here
    view_ids = first_view + lax.broadcasted_iota(jnp.int32, intersection_ids.shape, 0)
    owners = (intersection_ids // own_count).reshape(-1)
    request = (view_ids * own_count + intersection_ids % own_count).reshape(-1).astype(jnp.float32)
    peer_index = lax.broadcasted_iota(jnp.int32, (1, devices), 1)
    owner_table = (owners[:, None] == peer_index).astype(jnp.float32)
    ranks = slot_ranks(owner_table).astype(jnp.int32)
    rank_table = (ranks[:, None] == lax.broadcasted_iota(jnp.int32, (1, capacity), 1)).astype(
        jnp.float32
    )
    send_ids = (
        jnp.einsum("sd,sc->dc", owner_table, request[:, None] * rank_table, precision=exact_mode)
        .astype(jnp.int32)
        .reshape(-1)
    )
    got_ids = lax.all_to_all(send_ids, ("view", "tile"), split_axis=0, concat_axis=0, tiled=True)
    answer = fetch_rows(flat_rec, got_ids)
    fetched = lax.all_to_all(answer, ("view", "tile"), split_axis=1, concat_axis=1, tiled=True)
    by_rank = jnp.einsum(
        "kdc,sc->kds", fetched.reshape(9, devices, capacity), rank_table, precision=exact_mode
    )
    slot_rec = jnp.sum(by_rank * jnp.transpose(owner_table)[None], axis=1).reshape(
        9, views_here, tiles_here, slot_count
    )
    render_here = partial(render_all, order=depth_order, live_count=live_count)
    rendered, pullback = jax.vjp(render_here, slot_rec)
    slot_grad = pullback(rendered - target)[0].reshape(9, -1)
    weighted = slot_grad[:, :, None] * rank_table[None]
    back_buf = jnp.einsum("sd,ksc->kdc", owner_table, weighted, precision=exact_mode).reshape(
        9, devices * capacity
    )
    returned = lax.all_to_all(back_buf, ("view", "tile"), split_axis=1, concat_axis=1, tiled=True)
    record_grad = return_rows(returned, got_ids, rec_columns).reshape(records.shape)
    gradients = project_back(record_grad)
    return (rendered, gradients[0], gradients[1], gradients[2], gradients[3], next_owner)


def solution(mesh):
    in_specs = (
        P(None, ("view", "tile")),
        P(None, ("view", "tile")),
        P(("view", "tile")),
        P(None, ("view", "tile")),
        P(),
        P("view", "tile", None, None),
        P("view", "tile", None),
        P("view", "tile", None),
        P("view", "tile"),
    )
    out_specs = (
        P("view", "tile", None, None),
        P(None, ("view", "tile")),
        P(None, ("view", "tile")),
        P(("view", "tile")),
        P(None, ("view", "tile")),
        P("view", "tile"),
    )
    return jax.shard_map(shards, mesh=mesh, in_specs=in_specs, out_specs=out_specs, check_vma=False)
```

profile of v0, /device:TPU:1, one launch (start us, length us, event | category | flops | bytes accessed | tf_op | source)
XLA Modules:
  0.0 449.6 jit_solution(548986105920711819)
XLA Ops:
  2.0 1.8 fusion.101
  3.9 7.5 %fusion.125 = s32[128,128]{1,0:T(8,128)} fusion(f32[8192]{0:T(1024)S(1)} %bitcast.347, s32[8192]{0:T(1024)S(1)} %bitcast.327, s32[8192]{0:T(1024)S(1)} %bitcast.323), kind=kOutput, calls=%fused_computation.189 | convolution fusion | flops 1613774848 | bytes 163840 | tf_op jit(solution)/shard_map/sd,sc->dc/dot_general | solution.py:186
  11.4 11.9 %all-to-all-start = ((s32[128,128,1]{1,2,0:T(1,128)}), s32[128,128,1]{1,2,0:T(1,128)S(1)}, u32[]{:S(2)}, u32[]{:S(2)}) async-start(s32[128,128,1]{1,2,0:T(1,128)} %bitcast.15), calls=%async_computation | async-start | bytes 131072 | tf_op jit(solution)/shard_map/all_to_all | solution.py:190
  23.3 2.4 fusion.110
  25.8 5.0 %fusion.104 = f32[8192,128]{1,0:T(8,128)} fusion(s32[8192]{0:T(1024)S(1)} %bitcast.328), kind=kLoop, calls=%fused_computation.170 | loop fusion | flops 2097152 | bytes 4227072 | tf_op jit(solution)/shard_map/convert_element_type | solution.py:182
  32.9 2.6 copy.55
  37.3 56.6 %gather_fusion = f32[16384,9]{1,0:T(8,128)} fusion(f32[9,8192]{0,1:T(8,128)} %copy.55, s32[16384]{0:T(1024)S(1)} %broadcast_clamp_fusion), kind=kCustom, calls=%fused_computation | custom fusion | bytes 1245184 | tf_op jit(solution)/shard_map/jit(_take)/gather | solution.py:139
  93.9 5.2 %copy.56 = f32[9,128,128]{2,0,1:T(8,128)S(1)} copy(f32[9,128,128]{0,2,1:T(8,128)} %bitcast.306) | data formatting | bytes 1179648 | tf_op jit(solution)/shard_map/jit(_take)/gather | solution.py:139
  100.2 9.8 %all-to-all-start.1 = ((f32[9,128,128]{2,0,1:T(8,128)}), f32[9,128,128]{2,0,1:T(8,128)S(1)}, u32[]{:S(2)}, u32[]{:S(2)}) async-start(f32[9,128,128]{2,0,1:T(8,128)} %broadcast_select_fusion.2), calls=%async_computation.1 | async-start | bytes 2097152 | tf_op jit(solution)/shard_map/all_to_all | solution.py:192
  110.0 1.4 fusion.178
  111.4 20.2 %all-reduce.24 = (s32[2]{0:T(128)S(1)}, s32[64]{0:T(128)S(1)}) all-reduce(s32[2]{0:T(128)S(1)} %reduce_sum.229, s32[64]{0:T(128)S(1)} %dynamic-update-slice), channel_id=1, replica_groups=mesh['view'=4,'tile'=32] {'tile'}, use_global_device_ids=true, to_apply=%region_26.27 | all-reduce | flops 66 | bytes 528 | tf_op jit(solution)/shard_map/psum | solution.py:168
  131.7 5.6 %copy.65 = f32[8192,128]{0,1:T(8,128)} copy(f32[8192,128]{1,0:T(8,128)} %fusion.104) | data formatting | bytes 8388608 | tf_op jit(solution)/shard_map/convert_element_type | solution.py:182
  137.5 18.2 %multiply_reduce_fusion.1 = f32[9,8192]{1,0:T(8,128)S(1)} fusion(f32[128,8192]{1,0:T(8,128)} %fusion.110, s32[8192]{0:T(1024)S(1)} %bitcast.329, f32[9,128,128]{2,0,1:T(8,128)S(1)} %all-to-all-done.1), kind=kOutput, calls=%fused_computation.152 | convolution fusion | flops 14515363840 | bytes 5111808 | tf_op jit(solution)/shard_map/kdc,sc->kds/dot_general | solution.py:193
  156.4 30.5 %while.41 = (s32[]{:T(128)}, f32[4,8,3,256]{3,1,0,2:T(8,128)S(1)}, f32[4,8,9,256]{3,2,1,0:T(8,128)S(1)}, s32[4,8,256]{2,1,0:T(8,128)S(1)}, s32[4,8]{1,0:T(4,128)S(1)}, /*index=5*/s32[]{:T(128)}) while((s32[]{:T(128)}, f32[4,8,3,256]{3,1,0,2:T(8,128)S(1)}, f32[4,8,9,256]{3,2,1,0:T(8,128)S(1)}, s32[4,8,256]{2,1,0:T(8,128)S(1)}, ...), condition=%wide.region_8.9_spmd.clone, body=%wide.region_7.8_spmd.clone.sunk | while | flops 1700407296 | bytes 4864185 | solution.py:114
  157.8 3.3 fusion.234
  161.1 2.9 fusion.235
  164.0 1.3 fusion.231
  165.5 3.3 fusion.234
  168.7 2.9 fusion.235
  173.1 3.3 fusion.234
  176.4 2.9 fusion.235
  180.7 3.3 fusion.234
  184.0 2.9 fusion.235
  187.0 69.9 %while.40 = (s32[]{:T(128)}, f32[4,8,9,256]{3,2,1,0:T(8,128)S(1)}, f32[4,8,9,256]{3,2,1,0:T(8,128)S(1)}, s32[4,8,256]{2,1,0:T(8,128)S(1)}, s32[4,8]{1,0:T(4,128)...) while((s32[]{:T(128)}, f32[4,8,9,256]{3,2,1,0:T(8,128)S(1)}, ...), condition=%wide.region_16.17_spmd, body=%wide.region_9.16_spmd.sunk | while | flops 3417032704 | bytes 11907285 | solution.py:114
  196.7 2.7 fusion.221
  199.5 2.3 fusion.223
  201.8 1.9 fusion.220
  203.6 5.9 %fusion.222 = (f32[8,256]{1,0:T(8,128)S(1)}, f32[8,256]{1,0:T(8,128)S(1)}, f32[8,256]{1,0:T(8,128)S(1)}, f32[8,256]{1,0:T(8,128)S(1)}, f32[8,256]{1,0:T(8,128)S(1)}, /*index=5*/f32[8,256]{1,0:T(8,128)S(1)}) fusion(f32[8,256]{1,0:T(8,128)S(1)} %get-tuple-element.599, f32[256]{0:T(256)S(1)} %get-tuple-element.600, ...), kind=kOutput, calls=%fused_computation.30.clone.1 | convolution fusion | flops 1640550400 | bytes 4294656 | tf_op jit(solution)/shard_map/transpose(jvp())/while/body/eval_jaxpr/checkpoint/vmap()/dot_general | solution.py:91
  212.2 2.7 fusion.221
  214.9 2.3 fusion.223
  217.2 1.9 fusion.220
  219.1 5.9 %fusion.222 = (f32[8,256]{1,0:T(8,128)S(1)}, f32[8,256]{1,0:T(8,128)S(1)}, f32[8,256]{1,0:T(8,128)S(1)}, f32[8,256]{1,0:T(8,128)S(1)}, f32[8,256]{1,0:T(8,128)S(1)}, /*index=5*/f32[8,256]{1,0:T(8,128)S(1)}) fusion(f32[8,256]{1,0:T(8,128)S(1)} %get-tuple-element.599, f32[256]{0:T(256)S(1)} %get-tuple-element.600, ...), kind=kOutput, calls=%fused_computation.30.clone.1 | convolution fusion | flops 1640550400 | bytes 4294656 | tf_op jit(solution)/shard_map/transpose(jvp())/while/body/eval_jaxpr/checkpoint/vmap()/dot_general | solution.py:91
  227.6 2.7 fusion.221
  230.3 2.3 fusion.223
  232.6 1.9 fusion.220
  234.5 5.9 %fusion.222 = (f32[8,256]{1,0:T(8,128)S(1)}, f32[8,256]{1,0:T(8,128)S(1)}, f32[8,256]{1,0:T(8,128)S(1)}, f32[8,256]{1,0:T(8,128)S(1)}, f32[8,256]{1,0:T(8,128)S(1)}, /*index=5*/f32[8,256]{1,0:T(8,128)S(1)}) fusion(f32[8,256]{1,0:T(8,128)S(1)} %get-tuple-element.599, f32[256]{0:T(256)S(1)} %get-tuple-element.600, ...), kind=kOutput, calls=%fused_computation.30.clone.1 | convolution fusion | flops 1640550400 | bytes 4294656 | tf_op jit(solution)/shard_map/transpose(jvp())/while/body/eval_jaxpr/checkpoint/vmap()/dot_general | solution.py:91
  243.0 2.7 fusion.221
  245.8 2.3 fusion.223
  248.1 1.9 fusion.220
  250.0 5.9 %fusion.222 = (f32[8,256]{1,0:T(8,128)S(1)}, f32[8,256]{1,0:T(8,128)S(1)}, f32[8,256]{1,0:T(8,128)S(1)}, f32[8,256]{1,0:T(8,128)S(1)}, f32[8,256]{1,0:T(8,128)S(1)}, /*index=5*/f32[8,256]{1,0:T(8,128)S(1)}) fusion(f32[8,256]{1,0:T(8,128)S(1)} %get-tuple-element.599, f32[256]{0:T(256)S(1)} %get-tuple-element.600, ...), kind=kOutput, calls=%fused_computation.30.clone.1 | convolution fusion | flops 1640550400 | bytes 4294656 | tf_op jit(solution)/shard_map/transpose(jvp())/while/body/eval_jaxpr/checkpoint/vmap()/dot_general | solution.py:91
  257.5 20.5 %fusion.120 = f32[9,128,128]{1,2,0:T(8,128)S(1)} fusion(f32[8192,128]{0,1:T(8,128)} %copy.65, f32[9,8192]{1,0:T(8,128)S(1)} %bitcast.318, pred[8192,128,1]{1,0,2:T(32,128)(4,1)S(1)} %fusion.178), kind=kOutput, calls=%fused_computation.187 | convolution fusion | flops 14504951808 | bytes 6127616 | tf_op jit(solution)/shard_map/sd,ksc->kdc/dot_general | solution.py:203
  278.0 1.4 copy.66
  279.4 8.5 %all-to-all-start.2 = ((f32[9,128,128]{2,0,1:T(8,128)}), f32[9,128,128]{2,0,1:T(8,128)S(1)}, u32[]{:S(2)}, u32[]{:S(2)}) async-start(f32[9,128,128]{2,0,1:T(8,128)} %copy.66), calls=%async_computation.2 | async-start | bytes 2097152 | tf_op jit(solution)/shard_map/all_to_all | solution.py:206
  287.9 1.3 while.42
  290.8 15.9 %all-to-all-done.2 = f32[9,128,128]{2,0,1:T(8,128)S(1)} async-done(((f32[9,128,128]{2,0,1:T(8,128)}), f32[9,128,128]{2,0,1:T(8,128)S(1)}, u32[]{:S(2)}, u32[]{:S(2)}) %all-to-all-start.2) | async-done | bytes 589856 | tf_op jit(solution)/shard_map/all_to_all | solution.py:206
  307.6 4.7 %copy.68 = f32[16384,9]{1,0:T(8,128)} copy(f32[16384,9]{0,1:T(8,128)S(1)} %bitcast.307) | data formatting | bytes 1179648 | tf_op jit(solution)/shard_map/transpose | solution.py:143
  312.2 100.1 %scatter_custom_fusion = f32[8192,9]{1,0:T(8,128)} fusion(s32[16384]{0:T(1024)S(1)} %bitcast.317, f32[16384,9]{1,0:T(8,128)} %copy.68, f32[]{:T(128)} %constant.272.clone.1), kind=kCustom, calls=%fused_computation.178 | custom fusion | flops 147456 | bytes 295424 | tf_op jit(solution)/shard_map/scatter-add | solution.py:143
  412.3 32.5 %slice_reduce_fusion.2 = (f32[8192]{0:T(1024)S(1)}, f32[8192]{0:T(1024)S(1)}, f32[8192]{0:T(1024)S(1)}, f32[8192]{0:T(1024)S(1)}, f32[8192]{0:T(1024)S(1)}, /*in...) fusion(f32[9,8192]{0,1:T(8,128)} %bitcast.305), kind=kLoop, calls=%fused_computation.157 | loop fusion | bytes 589824 | tf_op jit(solution)/shard_map/transpose(jvp())/unstack | solution.py:60
  (280 shorter events, 28.6 us)
Async XLA Ops:
  0.6 31.1 %copy-start = (f32[3,1024]{1,0:T(4,128)S(1)}, f32[3,1024]{1,0:T(4,128)}, u32[]{:S(2)}) copy-start(f32[3,1024]{1,0:T(4,128)} %param.15) | copy-start | bytes 36868
  3.9 19.4 %copy-start.13 = (f32[6,1024]{1,0:T(8,128)S(1)}, f32[6,1024]{1,0:T(8,128)}, u32[]{:S(2)}) copy-start(f32[6,1024]{1,0:T(8,128)} %param.16) | copy-start | bytes 73732
  11.4 25.8 %all-to-all-start = ((s32[128,128,1]{1,2,0:T(1,128)}), s32[128,128,1]{1,2,0:T(1,128)S(1)}, u32[]{:S(2)}, u32[]{:S(2)}) async-start(s32[128,128,1]{1,2,0:T(1,128)} %bitcast.15), calls=%async_computation | async-start | bytes 131072 | tf_op jit(solution)/shard_map/all_to_all | solution.py:190
  25.7 5.3 %copy-start.11 = (f32[8,2,4]{0,2,1:T(4,128)S(1)}, f32[8,2,4]{0,2,1:T(4,128)}, u32[]{:S(2)}) copy-start(f32[8,2,4]{0,2,1:T(4,128)} %param.19) | copy-start | bytes 772
  25.7 5.9 %copy-start.17 = (f32[3,1024]{1,0:T(4,128)S(1)}, f32[3,1024]{1,0:T(4,128)}, u32[]{:S(2)}) copy-start(f32[3,1024]{1,0:T(4,128)} %param.18) | copy-start | bytes 36868
  25.7 6.3 %copy-start.14 = (f32[1024]{0:T(1024)S(1)}, f32[1024]{0:T(1024)}, u32[]{:S(2)}) copy-start(f32[1024]{0:T(1024)} %param.17) | copy-start | bytes 12292
  31.4 1.0 copy-start.1
  31.4 1.0 copy-start.4
  31.4 1.0 copy-start.6
  31.5 1.0 copy-start.8
  32.9 2.6 copy-start.18
  32.9 3.9 copy-start.16
  100.2 37.2 %all-to-all-start.1 = ((f32[9,128,128]{2,0,1:T(8,128)}), f32[9,128,128]{2,0,1:T(8,128)S(1)}, u32[]{:S(2)}, u32[]{:S(2)}) async-start(f32[9,128,128]{2,0,1:T(8,128)} %broadcast_select_fusion.2), calls=%async_computation.1 | async-start | bytes 2097152 | tf_op jit(solution)/shard_map/all_to_all | solution.py:192
  155.7 0.8 copy-start.3
  156.4 30.5 %copy-start.10 = (f32[2,16,3,256]{3,1,2,0:T(8,128)S(1)}, f32[2,16,3,256]{3,1,2,0:T(8,128)}, u32[]{:S(2)}) copy-start(f32[2,16,3,256]{3,1,2,0:T(8,128)} %param.20) | copy-start | bytes 294916
  279.4 27.3 %all-to-all-start.2 = ((f32[9,128,128]{2,0,1:T(8,128)}), f32[9,128,128]{2,0,1:T(8,128)S(1)}, u32[]{:S(2)}, u32[]{:S(2)}) async-start(f32[9,128,128]{2,0,1:T(8,128)} %copy.66), calls=%async_computation.2 | async-start | bytes 2097152 | tf_op jit(solution)/shard_map/all_to_all | solution.py:206
  412.3 32.6 %copy-start.5 = (f32[8,1024]{1,0:T(8,128)S(1)}, f32[8,1024]{1,0:T(8,128)}, u32[]{:S(2)}) copy-start(f32[8,1024]{1,0:T(8,128)} %copy-done.4) | copy-start | bytes 98308
  412.3 32.6 %copy-start.7 = (f32[8,1024]{1,0:T(8,128)S(1)}, f32[8,1024]{1,0:T(8,128)}, u32[]{:S(2)}) copy-start(f32[8,1024]{1,0:T(8,128)} %copy-done.6) | copy-start | bytes 98308
  412.3 32.6 %copy-start.9 = (f32[8,1024]{1,0:T(8,128)S(1)}, f32[8,1024]{1,0:T(8,128)}, u32[]{:S(2)}) copy-start(f32[8,1024]{1,0:T(8,128)} %copy-done.8) | copy-start | bytes 98308
  412.3 32.6 %copy-start.2 = (f32[8,2,3,1024]{3,0,1,2:T(8,128)S(1)}, f32[8,2,3,1024]{3,0,1,2:T(8,128)}, u32[]{:S(2)}) copy-start(f32[8,2,3,1024]{3,0,1,2:T(8,128)} %copy-done.1) | copy-start | bytes 589828
  412.3 32.7 %copy-start.12 = (f32[8,2,4]{0,2,1:T(4,128)S(1)}, f32[8,2,4]{0,2,1:T(4,128)}, u32[]{:S(2)}) copy-start(f32[8,2,4]{0,2,1:T(4,128)} %param.19) | copy-start | bytes 772
  444.8 1.6 copy-start.15
where the time goes:
time: 458 us; the launch traced here: 450 us
  matrix products  140 us (31%)
  other arithmetic  117 us (26%)
  local copies, waits for them, and re-layouts  114 us (25%)
  starting transfers between devices  30.1 us (7%)
  blocking collectives  20.2 us (4%)
  waiting for transfers between devices  15.9 us (3%)
  loops' own time  9.77 us (2%)
    scatter-add x1, other arithmetic, return_rows(): jax.ops.segment_sum(jnp.transpose(values), wanted, num_segments=columns)  100 us
    gather x2, local copies, waits for them, and re-layouts, fetch_rows(): return jnp.take(flat_rec, wanted, axis=1)  61.8 us
    dot_general x12, matrix products, render_tile(): through = jnp.exp(jnp.dot(keep_log, earlier, precision=exact_mode))  47.6 us
    another operation x10, local copies, waits for them, and re-layouts, project(): return jnp.stack(fields)  35.6 us
    dot_general x12, matrix products, render_tile(): return jnp.einsum('ck,pk->cp', ordered[6:9], weights, precision=exact_mode)  28.1 us
    dot_general x1, matrix products, shards(): jnp.einsum('sd,ksc->kdc', owner_table, weighted, precision=exact_mode)  20.5 us
    psum x1, blocking collectives, shards(): whole = lax.psum(totals, 'tile')  20.2 us
    dot_general x1, matrix products, shards(): jnp.einsum('kdc,sc->kds', fetched.reshape(9, devices, capacity), rank_tab...  18.2 us
  transfers between devices with their start and end apart: 3, of which 1 were waited for; matrix products, arithmetic and copies ran while one was open for 5% of the time, Pallas kernels for 0%

commit v1 on v0

v1 whole, which is shorter than its diff:
```python
from functools import partial

import jax
import jax.numpy as jnp
from jax import lax
from jax.experimental import pallas as pl
from jax.experimental.pallas import tpu as pltpu
from jax.sharding import PartitionSpec as P

SIDE = 16
PIX = SIDE * SIDE
LANES = 128
LANE_BITS = 7
ROWS = 8
FIELDS = 9
MOVING = 5
F32 = jnp.float32
BF16 = jnp.bfloat16
I32 = jnp.int32


def lanes(table, index):
    return jnp.take_along_axis(table, index, axis=1, mode="promise_in_bounds")


def iota(shape, axis):
    return lax.broadcasted_iota(I32, shape, axis)


def spread(row, count):
    return jnp.broadcast_to(row, (count, row.shape[1]))


def halves(array):
    high = array.astype(BF16)
    return high, (array - high.astype(F32)).astype(BF16)


def dot_nn(a, b):
    return lax.dot_general(a, b, (((1,), (0,)), ((), ())), preferred_element_type=F32)


def dot_nt(a, b):
    return lax.dot_general(a, b, (((1,), (1,)), ((), ())), preferred_element_type=F32)


def dot_tn(a, b):
    return lax.dot_general(a, b, (((0,), (0,)), ((), ())), preferred_element_type=F32)


def route_kernel(own_count, ids_ref, order_ref, live_ref, send_ref, inverse_ref, owner_ref, rank_ref, value_ref, acc_ref):
    tiles, slots = ids_ref.shape
    own_bits = own_count.bit_length() - 1
    devices = acc_ref.shape[0] // 4
    blocks = slots // LANES
    local_view = (iota((tiles, LANES), 0) >= tiles // 2).astype(I32)
    for block in range(blocks):
        here = slice(block * LANES, (block + 1) * LANES)
        order = order_ref[:, here]
        low, high = order & (LANES - 1), order >> LANE_BITS
        picked = jnp.zeros((tiles, LANES), I32)
        for source in range(blocks):
            found = lanes(ids_ref[:, source * LANES : (source + 1) * LANES], low)
            picked = jnp.where(high == source, found, picked)
        owner = jnp.where(order < live_ref[...], picked >> own_bits, -1)
        value = (picked & (own_count - 1)) + local_view * own_count
        for t in range(tiles):
            owner_ref[t, :, here] = owner[t : t + 1, :]
            value_ref[t, :, here] = value[t : t + 1, :]
    upto = (iota((slots, slots), 0) <= iota((slots, slots), 1)).astype(BF16)
    acc_ref[...] = jnp.zeros_like(acc_ref)
    peers = iota((devices, slots), 0)
    ranks = iota((LANES, slots), 0)
    place = iota((1, slots), 1)

    def tile(t, before):
        owner = owner_ref[t]
        value = value_ref[t]
        named = peers == owner
        count = dot_nn(named.astype(BF16), upto)
        rank = jnp.sum(jnp.where(named, count + before, 0.0), axis=0, keepdims=True) - 1.0
        rank = rank.astype(I32)
        rank_ref[t] = rank
        at_rank = (ranks == rank).astype(BF16)
        parts = [
            (value & 255).astype(F32),
            (value >> 8).astype(F32),
            place.astype(F32),
            jnp.full((1, slots), t + 1).astype(F32),
        ]
        left = jnp.concatenate([jnp.where(named, part, 0.0).astype(BF16) for part in parts], axis=0)
        acc_ref[...] += dot_nt(left, at_rank)
        return before + count[:, slots - 1 :]

    lax.fori_loop(0, tiles, tile, jnp.zeros((devices, 1), F32))
    part = [acc_ref[n * devices : (n + 1) * devices, :].astype(I32) for n in range(4)]
    send_ref[...] = part[0] + 256 * part[1]
    inverse_ref[...] = part[2] + 256 * (part[3] - 1)


def field_of(ref, row):
    return jnp.concatenate([ref[row : row + 1, h * LANES : (h + 1) * LANES] for h in range(ROWS)], axis=0)


def moving_fields(centres, shape_raw, view):
    rows = [view[0:4], view[4:8]]
    e0, e2, e5 = jnp.exp(shape_raw[0]), jnp.exp(shape_raw[2]), jnp.exp(shape_raw[5])
    screen, factor = [], []
    for m in rows:
        screen.append(m[0] * centres[0] + m[1] * centres[1] + m[2] * centres[2] + m[3])
        factor.append(
            (
                m[0] * e0 + m[1] * shape_raw[1] + m[2] * shape_raw[3],
                m[1] * e2 + m[2] * shape_raw[4],
                m[2] * e5,
            )
        )
    fx, fy = factor
    var_x = fx[0] * fx[0] + fx[1] * fx[1] + fx[2] * fx[2] + 0.3
    cov_xy = fx[0] * fy[0] + fx[1] * fy[1] + fx[2] * fy[2]
    var_y = fy[0] * fy[0] + fy[1] * fy[1] + fy[2] * fy[2] + 0.3
    inverse = 1.0 / (var_x * var_y - cov_xy * cov_xy)
    return screen[0], screen[1], var_y * inverse, -cov_xy * inverse, var_x * inverse


def opacity_of(logit):
    return 0.95 / (1.0 + jnp.exp(-logit))


def camera_view(camera_ref, view):
    return [camera_ref[view * 8 + n] for n in range(8)]


def answer_kernel(views, here, centres_ref, shape_ref, logit_ref, colours_ref, camera_ref, got_ref, out_ref, moving_ref, fixed_ref):
    centres = [field_of(centres_ref, n) for n in range(3)]
    shape_raw = [field_of(shape_ref, n) for n in range(6)]
    for view in range(views):
        found = moving_fields(centres, shape_raw, camera_view(camera_ref, view))
        for k in range(MOVING):
            moving_ref[view // here, k, (view % here) * ROWS : (view % here + 1) * ROWS, :] = found[k]
    fixed_ref[0] = opacity_of(logit_ref[...])
    for n in range(3):
        fixed_ref[1 + n] = field_of(colours_ref, n)
    devices = got_ref.shape[0]
    per_group = devices // (views // here) // ROWS

    def block(n, carry):
        row = pl.multiple_of(n * ROWS, ROWS)
        group = n // per_group
        ids = got_ref[pl.ds(row, ROWS), 0:LANES]
        low, high = ids & (LANES - 1), ids >> LANE_BITS
        high_fixed = high & (ROWS - 1)
        for k in range(FIELDS):
            moves = k < MOVING
            total = jnp.zeros((ROWS, LANES), F32)
            for h in range(ROWS * here if moves else ROWS):
                line = moving_ref[group, k, h : h + 1, :] if moves else fixed_ref[k - MOVING, h : h + 1, :]
                total = jnp.where((high if moves else high_fixed) == h, lanes(spread(line, ROWS), low), total)
            out_ref[pl.ds(row, ROWS), k * LANES : (k + 1) * LANES] = total
        return carry

    lax.fori_loop(0, devices // ROWS, block, 0)


def back_kernel(
    views, here, centres_ref, shape_ref, logit_ref, colours_ref, camera_ref, got_ref, given_ref,
    d_centres_ref, d_shape_ref, d_logit_ref, d_colours_ref, moving_ref, fixed_ref,
):
    devices = got_ref.shape[0]
    groups = views // here
    moving_ref[...] = jnp.zeros_like(moving_ref)
    fixed_ref[...] = jnp.zeros_like(fixed_ref)
    wide = ROWS * here
    per_step = 2

    def block(n, carry):
        row = pl.multiple_of(n * ROWS, ROWS)
        group = n // (devices // groups // ROWS)
        ids = got_ref[pl.ds(row, ROWS), 0:LANES]
        values = [given_ref[pl.ds(row, ROWS), k * LANES : (k + 1) * LANES] for k in range(FIELDS)]
        total = None
        for first in range(0, ROWS, per_step):
            lefts, onehots = [], []
            for src in range(first, first + per_step):
                low, high = ids[src : src + 1] & (LANES - 1), ids[src : src + 1] >> LANE_BITS
                at_wide = iota((wide, LANES), 0) == high
                at_row = iota((ROWS, LANES), 0) == (high & (ROWS - 1))
                rows = [
                    jnp.where(at_wide if k < MOVING else at_row, values[k][src : src + 1], 0.0)
                    for k in range(FIELDS)
                ]
                lefts.append(jnp.concatenate(rows, axis=0))
                onehots.append((iota((LANES, LANES), 0) == low).astype(BF16))
            left_high, left_low = halves(jnp.concatenate(lefts, axis=1))
            right = jnp.concatenate(onehots, axis=1)
            found = dot_nt(left_high, right) + dot_nt(left_low, right)
            total = found if total is None else total + found
        moving_ref[group] += total[: MOVING * wide]
        fixed_ref[...] += total[MOVING * wide :]
        return carry

    lax.fori_loop(0, devices // ROWS, block, 0)

    centres = [field_of(centres_ref, n) for n in range(3)]
    shape_raw = [field_of(shape_ref, n) for n in range(6)]
    d_centres = [jnp.zeros((ROWS, LANES), F32)] * 3
    d_shape = [jnp.zeros((ROWS, LANES), F32)] * 6
    for view in range(views):
        camera = camera_view(camera_ref, view)
        _, pull = jax.vjp(lambda c, s: moving_fields(c, s, camera), centres, shape_raw)
        base = (view % here) * ROWS
        given = tuple(
            moving_ref[view // here, k * wide + base : k * wide + base + ROWS, :] for k in range(MOVING)
        )
        more_centres, more_shape = pull(given)
        d_centres = [a + b for a, b in zip(d_centres, more_centres)]
        d_shape = [a + b for a, b in zip(d_shape, more_shape)]

    def put(ref, row, value):
        for h in range(ROWS):
            ref[row : row + 1, h * LANES : (h + 1) * LANES] = value[h : h + 1, :]

    for n in range(3):
        put(d_centres_ref, n, d_centres[n])
        put(d_colours_ref, n, fixed_ref[(1 + n) * ROWS : (2 + n) * ROWS, :])
    for n in range(6):
        put(d_shape_ref, n, d_shape[n])
    _, pull = jax.vjp(opacity_of, logit_ref[...])
    d_logit_ref[...] = pull(fixed_ref[0:ROWS, :])[0]


def render_kernel(
    recv_ref, owner_ref, rank_ref, inverse_ref, target_ref, image_ref, back_ref,
    cov_ref, high_ref, low_ref, dots_ref, grad_ref,
):
    tiles, _, slots = owner_ref.shape
    devices = recv_ref.shape[0]
    blocks = slots // LANES
    half = (SIDE - 1) / 2.0
    log2e = 1.4426950408889634
    before = (iota((slots, slots), 0) < iota((slots, slots), 1)).astype(BF16)
    after = (iota((slots, slots), 0) > iota((slots, slots), 1)).astype(BF16)
    across = iota((SIDE, slots), 0).astype(F32) - half
    sublane = iota((ROWS, LANES), 0)

    def fetch(t, block):
        here = slice(block * LANES, (block + 1) * LANES)
        owner = spread(owner_ref[t, :, here], ROWS) - sublane
        rank = spread(jnp.maximum(rank_ref[t, :, here], 0), ROWS)
        total = [jnp.zeros((ROWS, LANES), F32)] * FIELDS
        for group in range(devices // ROWS):
            mine = owner == group * ROWS
            for k in range(FIELDS):
                table = recv_ref[group * ROWS : (group + 1) * ROWS, k * LANES : (k + 1) * LANES]
                total[k] = jnp.where(mine, lanes(table, rank), total[k])
        return [jnp.sum(one, axis=0, keepdims=True) for one in total]

    def tile(t, carry):
        found = [fetch(t, block) for block in range(blocks)]
        u, w, a, b, c, opacity, red, green, blue = (
            jnp.concatenate([found[block][k] for block in range(blocks)], axis=1) for k in range(FIELDS)
        )
        dx = across - u
        scale = -0.5 * log2e
        first = (scale * a) * dx * dx
        second = (2.0 * scale * b) * dx
        third = scale * c
        for y in range(SIDE):
            rows = slice(y * SIDE, (y + 1) * SIDE)
            dy = (y - half) - w
            cover = opacity * jnp.exp2((second + third * dy) * dy + first)
            cov_ref[rows, :] = cover
            high, low = halves(jnp.log(1.0 - cover))
            high_ref[rows, :] = high
            low_ref[rows, :] = low
        through = jnp.exp(dot_nn(high_ref[...], before) + dot_nn(low_ref[...], before))
        weights = through * cov_ref[...]
        w_high, w_low = halves(weights)
        colour = jnp.concatenate([red, green, blue], axis=0)
        c_high = colour.astype(BF16).astype(F32)
        c_low = colour - c_high
        pair = jnp.concatenate([c_high, c_low], axis=0).astype(BF16)
        drawn = dot_nt(pair, w_high) + dot_nt(pair, w_low)
        image = drawn[0:3] + drawn[3:6]
        image_ref[t] = image
        error = image - target_ref[t]
        e_high = error.astype(BF16).astype(F32)
        e_low = error - e_high
        d_colour = jnp.concatenate([e_high, e_low], axis=0).astype(BF16)
        d_colour = dot_nn(d_colour, w_high) + dot_nn(d_colour, w_low)
        d_colour = d_colour[0:3] + d_colour[3:6]
        left = jnp.concatenate([e_high, e_high, e_low, e_low], axis=0).astype(BF16)
        right = jnp.concatenate([c_high, c_low, c_high, c_low], axis=0).astype(BF16)
        shade = dot_tn(left, right)
        s_high, s_low = halves(weights * shade)
        behind = dot_nn(s_high, after) + dot_nn(s_low, after)
        dots_ref[...] = through * shade * cov_ref[...] - behind * (cov_ref[...] / (1.0 - cov_ref[...]))
        sum0 = jnp.zeros((SIDE, slots), F32)
        sum1, sum2 = sum0, sum0
        for y in range(SIDE):
            given = dots_ref[y * SIDE : (y + 1) * SIDE, :]
            dy = (y - half) - w
            once = given * dy
            sum0, sum1, sum2 = sum0 + given, sum1 + once, sum2 + once * dy

        def down(x):
            return jnp.sum(x, axis=0, keepdims=True)

        once = sum0 * dx
        s0, sx, sxx = down(sum0), down(once), down(once * dx)
        sy, sxy, syy = down(sum1), down(sum1 * dx), down(sum2)
        grads = [
            a * sx + b * sy,
            b * sx + c * sy,
            -0.5 * sxx,
            -sxy,
            -0.5 * syy,
            jnp.where(opacity > 0.0, s0 / opacity, 0.0),
            d_colour[0:1],
            d_colour[1:2],
            d_colour[2:3],
        ]
        for k in range(FIELDS):
            for block in range(blocks):
                grad_ref[k, t * blocks + block] = grads[k][:, block * LANES : (block + 1) * LANES]
        return carry

    lax.fori_loop(0, tiles, tile, 0)

    def give(group, carry):
        row = pl.multiple_of(group * ROWS, ROWS)
        index = inverse_ref[pl.ds(row, ROWS), :]
        low = index & (LANES - 1)
        high = index >> LANE_BITS

        def step(h, totals):
            totals = list(totals)
            for half_step in range(blocks):
                place = h * blocks + half_step
                mine = high == place
                for k in range(FIELDS):
                    totals[k] = jnp.where(mine, lanes(spread(grad_ref[k, place], ROWS), low), totals[k])
            return tuple(totals)

        totals = lax.fori_loop(0, tiles, step, (jnp.zeros((ROWS, LANES), F32),) * FIELDS)
        for k in range(FIELDS):
            back_ref[pl.ds(row, ROWS), k * LANES : (k + 1) * LANES] = totals[k]
        return carry

    lax.fori_loop(0, devices // ROWS, give, 0)


VMEM = pl.BlockSpec(memory_space=pltpu.VMEM)
SMEM = pl.BlockSpec(memory_space=pltpu.SMEM)


def params():
    return pltpu.CompilerParams(vmem_limit_bytes=40 * 2**20)


def shape(dims, kind=F32):
    return jax.ShapeDtypeStruct(dims, kind)


def route(ids, order, live, devices, own_count):
    tiles, slots = ids.shape
    table = shape((devices, LANES), I32)
    return pl.pallas_call(
        partial(route_kernel, own_count),
        out_shape=(table, table, shape((tiles, 1, slots), I32), shape((tiles, 1, slots), I32)),
        in_specs=[VMEM] * 3,
        out_specs=(VMEM,) * 4,
        scratch_shapes=[pltpu.VMEM((tiles, 1, slots), I32), pltpu.VMEM((4 * devices, LANES), F32)],
        compiler_params=params(),
        name="route",
    )(ids, order, live)


def answer(centres, shape_raw, logit, colours, camera, got, views, here):
    return pl.pallas_call(
        partial(answer_kernel, views, here),
        out_shape=shape((got.shape[0], FIELDS * LANES)),
        in_specs=[VMEM] * 4 + [SMEM, VMEM],
        out_specs=VMEM,
        scratch_shapes=[
            pltpu.VMEM((views // here, MOVING, here * ROWS, LANES), F32),
            pltpu.VMEM((FIELDS - MOVING, ROWS, LANES), F32),
        ],
        compiler_params=params(),
        name="answer",
    )(centres, shape_raw, logit, colours, camera, got)


def render(recv, owner, rank, inverse, target):
    tiles, _, slots = owner.shape
    return pl.pallas_call(
        render_kernel,
        out_shape=(shape(target.shape), shape(recv.shape)),
        in_specs=[VMEM] * 5,
        out_specs=(VMEM, VMEM),
        scratch_shapes=[
            pltpu.VMEM((PIX, slots), F32),
            pltpu.VMEM((PIX, slots), BF16),
            pltpu.VMEM((PIX, slots), BF16),
            pltpu.VMEM((PIX, slots), F32),
            pltpu.VMEM((FIELDS, tiles * slots // LANES, 1, LANES), F32),
        ],
        compiler_params=params(),
        name="render",
    )(recv, owner, rank, inverse, target)


def back(centres, shape_raw, logit, colours, camera, got, given, views, here):
    return pl.pallas_call(
        partial(back_kernel, views, here),
        out_shape=(shape(centres.shape), shape(shape_raw.shape), shape(logit.shape), shape(colours.shape)),
        in_specs=[VMEM] * 4 + [SMEM, VMEM, VMEM],
        out_specs=(VMEM,) * 4,
        scratch_shapes=[
            pltpu.VMEM((views // here, MOVING * here * ROWS, LANES), F32),
            pltpu.VMEM(((FIELDS - MOVING) * ROWS, LANES), F32),
        ],
        compiler_params=params(),
        name="back",
    )(centres, shape_raw, logit, colours, camera, got, given)


def shards(centres, shape_raw, opacity_logit, colours, camera, target, intersection_ids, depth_order, live_count):
    view_group, tile_group = lax.axis_size("view"), lax.axis_size("tile")
    devices = view_group * tile_group
    own_count = centres.shape[1]
    here, tiles_here, slots = intersection_ids.shape
    views = camera.shape[0]
    tiles = here * tiles_here
    axes = ("view", "tile")
    exchange = partial(lax.all_to_all, axis_name=axes, split_axis=0, concat_axis=0, tiled=True)

    send, inverse, owner, rank = route(
        intersection_ids.reshape(tiles, slots),
        depth_order.reshape(tiles, slots),
        live_count.reshape(tiles, 1),
        devices,
        own_count,
    )
    totals = jnp.sum(live_count, axis=1)
    told = jnp.zeros((devices, LANES), I32).at[:, 0:here].set(totals[None, :])
    got = exchange(jnp.concatenate([send, told], axis=1))
    logit = opacity_logit.reshape(ROWS, LANES)
    flat_camera = camera.reshape(-1)
    answers = answer(centres, shape_raw, logit, colours, flat_camera, got, views, here)
    recv = exchange(answers)
    image, returned = render(recv, owner, rank, inverse, target.reshape(tiles, 3, PIX))
    given = exchange(returned)
    d_centres, d_shape, d_logit, d_colours = back(
        centres, shape_raw, logit, colours, flat_camera, got, given, views, here
    )

    me_view, me_tile = lax.axis_index("view"), lax.axis_index("tile")
    source = jnp.arange(devices, dtype=I32)[:, None]
    in_group = source // tile_group == me_view
    counts = got[:, LANES : LANES + here]
    whole = jnp.sum(jnp.where(in_group, counts, 0), axis=0)
    before = jnp.sum(jnp.where(in_group & (source % tile_group < me_tile), counts, 0), axis=0)
    earlier = jnp.arange(tiles_here)[:, None] < jnp.arange(tiles_here)[None, :]
    within = jnp.sum(jnp.where(earlier[None], live_count[:, :, None], 0), axis=1)
    next_owner = (before[:, None] + within) * tile_group // whole[:, None]
    return (
        image.reshape(target.shape),
        d_centres,
        d_shape,
        d_logit.reshape(opacity_logit.shape),
        d_colours,
        next_owner.astype(I32),
    )


def solution(mesh):
    in_specs = (
        P(None, ("view", "tile")),
        P(None, ("view", "tile")),
        P(("view", "tile")),
        P(None, ("view", "tile")),
        P(),
        P("view", "tile", None, None),
        P("view", "tile", None),
        P("view", "tile", None),
        P("view", "tile"),
    )
    out_specs = (
        P("view", "tile", None, None),
        P(None, ("view", "tile")),
        P(None, ("view", "tile")),
        P(("view", "tile")),
        P(None, ("view", "tile")),
        P("view", "tile"),
    )
    return jax.shard_map(shards, mesh=mesh, in_specs=in_specs, out_specs=out_specs, check_vma=False)
```

time: 458 us -> 178 us (0.39); the launches traced: 450 us -> 178 us
  matrix products: 140 us -> 0 us
  other arithmetic: 117 us -> 2.42 us
  Pallas kernels: 0 us -> 111 us
  local copies, waits for them, and re-layouts: 114 us -> 6.95 us
  waiting for transfers between devices: 15.9 us -> 36.4 us
  blocking collectives: 20.2 us -> 0 us
  starting transfers between devices: 30.1 us -> 20.2 us
  loops' own time: 9.77 us -> 0 us
    dot_general x44 -> x0, matrix products: 140 us -> none  [the longest x12 47.6 us: render_tile(): through = jnp.exp(jnp.dot(keep_log, earlier, precision=exact_mode))]
    pallas_call x0 -> x4, Pallas kernels: none -> 111 us  [the longest x1 86.5 us: render(): pl.pallas_call(render_kernel, out_shape=(shape(target.shape), shape(recv....]
    scatter-add x1 -> x0, other arithmetic: 100 us -> none  [return_rows(): jax.ops.segment_sum(jnp.transpose(values), wanted, num_segments=columns)]
    gather x2 -> x0, local copies, waits for them, and re-layouts: 61.8 us -> none  [fetch_rows(): return jnp.take(flat_rec, wanted, axis=1)]
    another operation x17 -> x0, local copies, waits for them, and re-layouts: 35.8 us -> none  [the longest x10 35.6 us: project(): return jnp.stack(fields)]
    all_to_all x3, waiting for transfers between devices: 15.9 us -> 36.4 us  [the longest x1 14.1 us: shards(): recv = exchange(answers)]
    psum x1 -> x0, blocking collectives: 20.2 us -> none  [shards(): whole = lax.psum(totals, 'tile')]
    all_to_all x3, starting transfers between devices: 30.1 us -> 20.2 us  [the longest x1 11.5 us: shards(): got = exchange(jnp.concatenate([send, told], axis=1))]
  transfers between devices with their start and end apart: 3 -> 3, of which waited for: 1 -> 3; matrix products, arithmetic and copies ran while one was open for 5% -> 1% of each run, Pallas kernels for 0% -> 0%
where the time goes in v1:
time: 178 us
  Pallas kernels  111 us (62%)
  waiting for transfers between devices  36.4 us (20%)
  starting transfers between devices  20.2 us (11%)
  local copies, waits for them, and re-layouts  6.95 us (4%)
  other arithmetic  2.42 us (1%)
    pallas_call x1, Pallas kernels, render(): pl.pallas_call(render_kernel, out_shape=(shape(target.shape), shape(recv....  86.5 us
    pallas_call x1, Pallas kernels, route(): pl.pallas_call(partial(route_kernel, own_count), out_shape=(table, table,...  14.3 us
    all_to_all x1, waiting for transfers between devices, shards(): recv = exchange(answers)  14.1 us
    all_to_all x1, waiting for transfers between devices, shards(): given = exchange(returned)  12.5 us
    all_to_all x1, starting transfers between devices, shards(): got = exchange(jnp.concatenate([send, told], axis=1))  11.5 us
    all_to_all x1, waiting for transfers between devices, shards(): got = exchange(jnp.concatenate([send, told], axis=1))  9.79 us
    pallas_call x1, Pallas kernels, back(): pl.pallas_call(partial(back_kernel, views, here), out_shape=(shape(centre...  6.42 us
    all_to_all x1, starting transfers between devices, shards(): given = exchange(returned)  4.63 us
  transfers between devices with their start and end apart: 3, of which 3 were waited for; matrix products, arithmetic and copies ran while one was open for 1% of the time, Pallas kernels for 0%

profile of v1, /device:TPU:1, one launch (start us, length us, event | category | flops | bytes accessed | tf_op | source)
XLA Modules:
  0.0 177.7 jit_solution(15510808261786680524)
XLA Ops:
  0.6 0.0 copy-start.7
  0.6 0.6 compare_reduce_fusion
  1.3 0.0 copy-done.7
  1.3 0.1 reshape.152.live_ref
  1.4 0.1 reduce_sum.36
  1.5 0.7 broadcast_select_fusion
  2.2 0.0 copy-start.3
  2.2 0.7 copy-done.3
  3.0 0.0 copy-start.4
  3.0 0.8 copy-done.4
  3.7 14.3 %route.1 = (s32[128,128]{1,0:T(8,128)S(1)}, s32[128,128]{1,0:T(8,128)S(1)}, s32[32,1,256]{2,1,0:T(1,128)S(1)}, s32[32,1,256]{2,1,0:T(1,128)S(1)}) custom-call(s32[32,256]{1,0:T(8,128)S(1)} %bitcast.28, s32[32,256]{1,0:T(8,128)S(1)} %bitcast.29, s32[32,1]{1,0:T(8,128)S(1)} %reshape.152.live_ref), custom_call_target="tpu_custom_call" | custom-call | tf_op jit(solution)/shard_map/route/pallas_call | solution.py:368
  18.0 0.8 copy.32
  18.8 0.0 copy-start.8
  18.8 11.5 %all-to-all-start = ((s32[128,1,256]{2,1,0:T(1,128)}), s32[128,1,256]{2,1,0:T(1,128)S(1)}, u32[]{:S(2)}, u32[]{:S(2)}) async-start(s32[128,1,256]{2,1,0:T(1,128)} %copy.32), calls=%async_computation | async-start | bytes 262144 | tf_op jit(solution)/shard_map/all_to_all | solution.py:447
  30.3 0.0 copy-done.8
  30.3 0.1 copy.30
  30.4 0.1 reshape.145.camera_ref
  30.5 0.0 copy-start
  30.5 0.0 copy-start.1
  30.5 0.0 copy-start.2
  30.5 9.8 %all-to-all-done = s32[128,1,256]{2,1,0:T(1,128)S(1)} async-done(((s32[128,1,256]{2,1,0:T(1,128)}), s32[128,1,256]{2,1,0:T(1,128)S(1)}, u32[]{:S(2)}, u32[]{:S(2)}) %all-to-all-start) | async-done | bytes 131104 | tf_op jit(solution)/shard_map/all_to_all | solution.py:447
  40.3 0.0 copy-start.5
  40.3 0.0 copy-done
  40.3 0.0 copy-done.1
  40.3 0.0 copy-done.2
  40.3 0.6 copy-done.5
  41.0 3.7 %answer.1 = f32[128,1152]{1,0:T(8,128)S(1)} custom-call(f32[3,1024]{1,0:T(4,128)S(1)} %copy-done.1, f32[6,1024]{1,0:T(8,128)S(1)} %copy-done, f32[8,128]{1,0:T(8,128)S(1)} %bitcast.30, f32[3,1024]{1,0:T(4,128)S(1)} %copy-done.2, f32[64]{0:T(128)S(1)} %reshape.145.camera_ref, s32[128,256]{1,0:T(8,128)S(1)} %bitcast.22), custom_call_target="tpu_custom_call" | custom-call | tf_op jit(solution)/shard_map/answer/pallas_call | solution.py:380
  44.7 1.4 copy.33
  46.1 0.0 copy-start.6
  46.1 4.1 %all-to-all-start.1 = ((f32[128,1,1152]{2,1,0:T(1,128)}), f32[128,1,1152]{2,1,0:T(1,128)S(1)}, u32[]{:S(2)}, u32[]{:S(2)}) async-start(f32[128,1,1152]{2,1,0:T(1,128)} %copy.33), calls=%async_computation.1 | async-start | bytes 1179648 | tf_op jit(solution)/shard_map/all_to_all | solution.py:451
  50.2 0.0 copy-done.6
  50.2 0.1 copy.34
  50.3 14.1 %all-to-all-done.1 = f32[128,1,1152]{2,1,0:T(1,128)S(1)} async-done(((f32[128,1,1152]{2,1,0:T(1,128)}), f32[128,1,1152]{2,1,0:T(1,128)S(1)}, u32[]{:S(2)}, u32[]{:S(2)}) %all-to-all-start.1) | async-done | bytes 589856 | tf_op jit(solution)/shard_map/all_to_all | solution.py:451
  64.4 86.5 %render.1 = (f32[32,3,256]{2,1,0:T(4,128)S(1)}, f32[128,1152]{1,0:T(8,128)S(1)}) custom-call(f32[128,1152]{1,0:T(8,128)S(1)} %bitcast.19, s32[32,1,256]{2,1,0:T(1,128)S(1)} %get-tuple-element.29.owner_ref, s32[32,1,256]{2,1,0:T(1,128)S(1)} %get-tuple-element.30.rank_ref, s32[128,128]{1,0:T(8,128)S(1)} %get-tuple-element.31.inverse_ref, ...), custom_call_target="tpu_custom_call" | custom-call | tf_op jit(solution)/shard_map/render/pallas_call | solution.py:396
  150.9 1.4 copy.35
  152.4 4.6 %all-to-all-start.2 = ((f32[128,1,1152]{2,1,0:T(1,128)}), f32[128,1,1152]{2,1,0:T(1,128)S(1)}, u32[]{:S(2)}, u32[]{:S(2)}) async-start(f32[128,1,1152]{2,1,0:T(1,128)} %copy.35), calls=%async_computation.2 | async-start | bytes 1179648 | tf_op jit(solution)/shard_map/all_to_all | solution.py:453
  157.0 0.1 select_reduce_fusion.2
  157.1 0.1 select_reduce_fusion.1
  157.2 0.8 and_select_fusion
  158.0 0.7 copy.36
  158.7 12.5 %all-to-all-done.2 = f32[128,1,1152]{2,1,0:T(1,128)S(1)} async-done(((f32[128,1,1152]{2,1,0:T(1,128)}), f32[128,1,1152]{2,1,0:T(1,128)S(1)}, u32[]{:S(2)}, u32[]{:S(2)}) %all-to-all-start.2) | async-done | bytes 589856 | tf_op jit(solution)/shard_map/all_to_all | solution.py:453
  171.2 6.4 %back.1 = (f32[3,1024]{1,0:T(4,128)}, f32[6,1024]{1,0:T(8,128)}, f32[8,128]{1,0:T(8,128)}, f32[3,1024]{1,0:T(4,128)}) custom-call(f32[3,1024]{1,0:T(4,128)S(1)} %copy-done.1, f32[6,1024]{1,0:T(8,128)S(1)} %copy-done, f32[8,128]{1,0:T(8,128)S(1)} %bitcast.31, f32[3,1024]{1,0:T(4,128)S(1)} %copy-done.2, f32[64]{0:T(128)S(1)} %reshape.145.camera_ref, ...), custom_call_target="tpu_custom_call" | custom-call | tf_op jit(solution)/shard_map/back/pallas_call | solution.py:414
  (8 shorter events, 0.1 us)
Async XLA Ops:
  0.6 0.7 copy-start.7
  2.2 0.8 copy-start.3
  3.0 0.8 copy-start.4
  18.8 11.5 %copy-start.8 = (f32[8,2,4]{0,2,1:T(4,128)S(1)}, f32[8,2,4]{0,2,1:T(4,128)}, u32[]{:S(2)}) copy-start(f32[8,2,4]{0,2,1:T(4,128)} %param.15) | copy-start | bytes 772
  18.8 21.5 %all-to-all-start = ((s32[128,1,256]{2,1,0:T(1,128)}), s32[128,1,256]{2,1,0:T(1,128)S(1)}, u32[]{:S(2)}, u32[]{:S(2)}) async-start(s32[128,1,256]{2,1,0:T(1,128)} %copy.32), calls=%async_computation | async-start | bytes 262144 | tf_op jit(solution)/shard_map/all_to_all | solution.py:447
  30.5 9.8 %copy-start = (f32[6,1024]{1,0:T(8,128)S(1)}, f32[6,1024]{1,0:T(8,128)}, u32[]{:S(2)}) copy-start(f32[6,1024]{1,0:T(8,128)} %shape_ref.3) | copy-start | bytes 73732
  30.5 9.8 %copy-start.1 = (f32[3,1024]{1,0:T(4,128)S(1)}, f32[3,1024]{1,0:T(4,128)}, u32[]{:S(2)}) copy-start(f32[3,1024]{1,0:T(4,128)} %centres_ref.3) | copy-start | bytes 36868
  30.5 9.8 %copy-start.2 = (f32[3,1024]{1,0:T(4,128)S(1)}, f32[3,1024]{1,0:T(4,128)}, u32[]{:S(2)}) copy-start(f32[3,1024]{1,0:T(4,128)} %colours_ref.3) | copy-start | bytes 36868
  40.3 0.7 copy-start.5
  46.1 4.1 %copy-start.6 = (f32[2,16,3,256]{3,1,2,0:T(8,128)S(1)}, f32[2,16,3,256]{3,1,2,0:T(8,128)}, u32[]{:S(2)}) copy-start(f32[2,16,3,256]{3,1,2,0:T(8,128)} %param.16) | copy-start | bytes 294916
  46.1 18.3 %all-to-all-start.1 = ((f32[128,1,1152]{2,1,0:T(1,128)}), f32[128,1,1152]{2,1,0:T(1,128)S(1)}, u32[]{:S(2)}, u32[]{:S(2)}) async-start(f32[128,1,1152]{2,1,0:T(1,128)} %copy.33), calls=%async_computation.1 | async-start | bytes 1179648 | tf_op jit(solution)/shard_map/all_to_all | solution.py:451
  152.4 18.8 %all-to-all-start.2 = ((f32[128,1,1152]{2,1,0:T(1,128)}), f32[128,1,1152]{2,1,0:T(1,128)S(1)}, u32[]{:S(2)}, u32[]{:S(2)}) async-start(f32[128,1,1152]{2,1,0:T(1,128)} %copy.35), calls=%async_computation.2 | async-start | bytes 1179648 | tf_op jit(solution)/shard_map/all_to_all | solution.py:453

commit v2 on v1

--- a/solution.py
+++ b/solution.py
@@ -14,6 +14,7 @@
 ROWS = 8
 FIELDS = 9
 MOVING = 5
+TOGETHER = 4
 F32 = jnp.float32
 BF16 = jnp.bfloat16
 I32 = jnp.int32
@@ -48,10 +49,10 @@
     return lax.dot_general(a, b, (((0,), (0,)), ((), ())), preferred_element_type=F32)
 
 
-def route_kernel(own_count, ids_ref, order_ref, live_ref, send_ref, inverse_ref, owner_ref, rank_ref, value_ref, acc_ref):
+def route_kernel(own_count, ids_ref, order_ref, live_ref, send_ref, owner_ref, rank_ref, value_ref, acc_ref):
     tiles, slots = ids_ref.shape
     own_bits = own_count.bit_length() - 1
-    devices = acc_ref.shape[0] // 4
+    devices = acc_ref.shape[0] // 2
     blocks = slots // LANES
     local_view = (iota((tiles, LANES), 0) >= tiles // 2).astype(I32)
     for block in range(blocks):
@@ -71,7 +72,6 @@
     acc_ref[...] = jnp.zeros_like(acc_ref)
     peers = iota((devices, slots), 0)
     ranks = iota((LANES, slots), 0)
-    place = iota((1, slots), 1)
 
     def tile(t, before):
         owner = owner_ref[t]
@@ -82,20 +82,14 @@
         rank = rank.astype(I32)
         rank_ref[t] = rank
         at_rank = (ranks == rank).astype(BF16)
-        parts = [
-            (value & 255).astype(F32),
-            (value >> 8).astype(F32),
-            place.astype(F32),
-            jnp.full((1, slots), t + 1).astype(F32),
-        ]
+        parts = [(value & 255).astype(F32), (value >> 8).astype(F32)]
         left = jnp.concatenate([jnp.where(named, part, 0.0).astype(BF16) for part in parts], axis=0)
         acc_ref[...] += dot_nt(left, at_rank)
         return before + count[:, slots - 1 :]
 
-    lax.fori_loop(0, tiles, tile, jnp.zeros((devices, 1), F32))
-    part = [acc_ref[n * devices : (n + 1) * devices, :].astype(I32) for n in range(4)]
-    send_ref[...] = part[0] + 256 * part[1]
-    inverse_ref[...] = part[2] + 256 * (part[3] - 1)
+    lax.fori_loop(0, tiles, tile, jnp.zeros((devices, 1), F32), unroll=8)
+    low, high = acc_ref[0:devices, :].astype(I32), acc_ref[devices:, :].astype(I32)
+    send_ref[...] = low + 256 * high
 
 
 def field_of(ref, row):
@@ -230,8 +224,8 @@
 
 
 def render_kernel(
-    recv_ref, owner_ref, rank_ref, inverse_ref, target_ref, image_ref, back_ref,
-    cov_ref, high_ref, low_ref, dots_ref, grad_ref,
+    recv_ref, owner_ref, rank_ref, target_ref, image_ref, back_ref,
+    cov_ref, odds_ref, high_ref, low_ref, dots_ref, acc_ref,
 ):
     tiles, _, slots = owner_ref.shape
     devices = recv_ref.shape[0]
@@ -242,6 +236,8 @@
     after = (iota((slots, slots), 0) > iota((slots, slots), 1)).astype(BF16)
     across = iota((SIDE, slots), 0).astype(F32) - half
     sublane = iota((ROWS, LANES), 0)
+    split = devices // 2
+    peers, places = iota((split, slots), 0), iota((2 * LANES, slots), 0)
 
     def fetch(t, block):
         here = slice(block * LANES, (block + 1) * LANES)
@@ -255,11 +251,15 @@
                 total[k] = jnp.where(mine, lanes(table, rank), total[k])
         return [jnp.sum(one, axis=0, keepdims=True) for one in total]
 
-    def tile(t, carry):
+    def tile(t, lane):
+        cov, odds, high_part, low_part, dots = (
+            ref.at[lane] for ref in (cov_ref, odds_ref, high_ref, low_ref, dots_ref)
+        )
         found = [fetch(t, block) for block in range(blocks)]
         u, w, a, b, c, opacity, red, green, blue = (
             jnp.concatenate([found[block][k] for block in range(blocks)], axis=1) for k in range(FIELDS)
         )
+        yield
         dx = across - u
         scale = -0.5 * log2e
         first = (scale * a) * dx * dx
@@ -269,13 +269,17 @@
             rows = slice(y * SIDE, (y + 1) * SIDE)
             dy = (y - half) - w
             cover = opacity * jnp.exp2((second + third * dy) * dy + first)
-            cov_ref[rows, :] = cover
-            high, low = halves(jnp.log(1.0 - cover))
-            high_ref[rows, :] = high
-            low_ref[rows, :] = low
-        through = jnp.exp(dot_nn(high_ref[...], before) + dot_nn(low_ref[...], before))
-        weights = through * cov_ref[...]
+            cov[rows, :] = cover
+            keep = jnp.log(1.0 - cover)
+            odds[rows, :] = cover * jnp.exp(-keep)
+            high, low = halves(keep)
+            high_part[rows, :] = high
+            low_part[rows, :] = low
+        yield
+        through = jnp.exp(dot_nn(high_part[...], before) + dot_nn(low_part[...], before))
+        weights = through * cov[...]
         w_high, w_low = halves(weights)
+        yield
         colour = jnp.concatenate([red, green, blue], axis=0)
         c_high = colour.astype(BF16).astype(F32)
         c_low = colour - c_high
@@ -289,16 +293,19 @@
         d_colour = jnp.concatenate([e_high, e_low], axis=0).astype(BF16)
         d_colour = dot_nn(d_colour, w_high) + dot_nn(d_colour, w_low)
         d_colour = d_colour[0:3] + d_colour[3:6]
-        left = jnp.concatenate([e_high, e_high, e_low, e_low], axis=0).astype(BF16)
-        right = jnp.concatenate([c_high, c_low, c_high, c_low], axis=0).astype(BF16)
-        shade = dot_tn(left, right)
-        s_high, s_low = halves(weights * shade)
+        yield
+        column = jnp.concatenate([error, jnp.zeros((ROWS - 3, PIX), F32)], axis=0).T
+        shade = column[:, 0:1] * red + column[:, 1:2] * green + column[:, 2:3] * blue
+        shaded = weights * shade
+        s_high, s_low = halves(shaded)
+        yield
         behind = dot_nn(s_high, after) + dot_nn(s_low, after)
-        dots_ref[...] = through * shade * cov_ref[...] - behind * (cov_ref[...] / (1.0 - cov_ref[...]))
+        dots[...] = shaded - behind * odds[...]
+        yield
         sum0 = jnp.zeros((SIDE, slots), F32)
         sum1, sum2 = sum0, sum0
         for y in range(SIDE):
-            given = dots_ref[y * SIDE : (y + 1) * SIDE, :]
+            given = dots[y * SIDE : (y + 1) * SIDE, :]
             dy = (y - half) - w
             once = given * dy
             sum0, sum1, sum2 = sum0 + given, sum1 + once, sum2 + once * dy
@@ -320,34 +327,28 @@
             d_colour[1:2],
             d_colour[2:3],
         ]
-        for k in range(FIELDS):
-            for block in range(blocks):
-                grad_ref[k, t * blocks + block] = grads[k][:, block * LANES : (block + 1) * LANES]
+        owner, rank = owner_ref[t], rank_ref[t]
+        yield
+        named = ((owner & (split - 1)) == peers).astype(BF16)
+        place = (owner >> (split.bit_length() - 1)) * LANES + rank == places
+        parts = [halves(grad) for grad in grads]
+        left = [jnp.concatenate([named * part[n] for part in parts], axis=0) for n in range(2)]
+        right = place.astype(BF16)
+        acc_ref[...] += dot_nt(jnp.concatenate(left, axis=1), jnp.concatenate([right, right], axis=1))
+
+    def together(n, carry):
+        running = [tile(n * TOGETHER + lane, lane) for lane in range(TOGETHER)]
+        while running:
+            running = [one for one in running if next(one, one) is None]
         return carry
 
-    lax.fori_loop(0, tiles, tile, 0)
-
-    def give(group, carry):
-        row = pl.multiple_of(group * ROWS, ROWS)
-        index = inverse_ref[pl.ds(row, ROWS), :]
-        low = index & (LANES - 1)
-        high = index >> LANE_BITS
-
-        def step(h, totals):
-            totals = list(totals)
-            for half_step in range(blocks):
-                place = h * blocks + half_step
-                mine = high == place
-                for k in range(FIELDS):
-                    totals[k] = jnp.where(mine, lanes(spread(grad_ref[k, place], ROWS), low), totals[k])
-            return tuple(totals)
-
-        totals = lax.fori_loop(0, tiles, step, (jnp.zeros((ROWS, LANES), F32),) * FIELDS)
-        for k in range(FIELDS):
-            back_ref[pl.ds(row, ROWS), k * LANES : (k + 1) * LANES] = totals[k]
-        return carry
-
-    lax.fori_loop(0, devices // ROWS, give, 0)
+    acc_ref[...] = jnp.zeros_like(acc_ref)
+    lax.fori_loop(0, tiles // TOGETHER, together, 0)
+    for k in range(FIELDS):
+        for n in range(2):
+            back_ref[n * split : (n + 1) * split, k * LANES : (k + 1) * LANES] = acc_ref[
+                k * split : (k + 1) * split, n * LANES : (n + 1) * LANES
+            ]
 
 
 VMEM = pl.BlockSpec(memory_space=pltpu.VMEM)
@@ -364,13 +365,12 @@
 
 def route(ids, order, live, devices, own_count):
     tiles, slots = ids.shape
-    table = shape((devices, LANES), I32)
     return pl.pallas_call(
         partial(route_kernel, own_count),
-        out_shape=(table, table, shape((tiles, 1, slots), I32), shape((tiles, 1, slots), I32)),
+        out_shape=(shape((devices, LANES), I32), shape((tiles, 1, slots), I32), shape((tiles, 1, slots), I32)),
         in_specs=[VMEM] * 3,
-        out_specs=(VMEM,) * 4,
-        scratch_shapes=[pltpu.VMEM((tiles, 1, slots), I32), pltpu.VMEM((4 * devices, LANES), F32)],
+        out_specs=(VMEM,) * 3,
+        scratch_shapes=[pltpu.VMEM((tiles, 1, slots), I32), pltpu.VMEM((2 * devices, LANES), F32)],
         compiler_params=params(),
         name="route",
     )(ids, order, live)
@@ -391,23 +391,24 @@
     )(centres, shape_raw, logit, colours, camera, got)
 
 
-def render(recv, owner, rank, inverse, target):
+def render(recv, owner, rank, target):
     tiles, _, slots = owner.shape
     return pl.pallas_call(
         render_kernel,
         out_shape=(shape(target.shape), shape(recv.shape)),
-        in_specs=[VMEM] * 5,
+        in_specs=[VMEM] * 4,
         out_specs=(VMEM, VMEM),
         scratch_shapes=[
-            pltpu.VMEM((PIX, slots), F32),
-            pltpu.VMEM((PIX, slots), BF16),
-            pltpu.VMEM((PIX, slots), BF16),
-            pltpu.VMEM((PIX, slots), F32),
-            pltpu.VMEM((FIELDS, tiles * slots // LANES, 1, LANES), F32),
+            pltpu.VMEM((TOGETHER, PIX, slots), F32),
+            pltpu.VMEM((TOGETHER, PIX, slots), F32),
+            pltpu.VMEM((TOGETHER, PIX, slots), BF16),
+            pltpu.VMEM((TOGETHER, PIX, slots), BF16),
+            pltpu.VMEM((TOGETHER, PIX, slots), F32),
+            pltpu.VMEM((FIELDS * recv.shape[0] // 2, 2 * LANES), F32),
         ],
         compiler_params=params(),
         name="render",
-    )(recv, owner, rank, inverse, target)
+    )(recv, owner, rank, target)
 
 
 def back(centres, shape_raw, logit, colours, camera, got, given, views, here):
@@ -435,7 +436,7 @@
     axes = ("view", "tile")
     exchange = partial(lax.all_to_all, axis_name=axes, split_axis=0, concat_axis=0, tiled=True)
 
-    send, inverse, owner, rank = route(
+    send, owner, rank = route(
         intersection_ids.reshape(tiles, slots),
         depth_order.reshape(tiles, slots),
         live_count.reshape(tiles, 1),
@@ -449,7 +450,7 @@
     flat_camera = camera.reshape(-1)
     answers = answer(centres, shape_raw, logit, colours, flat_camera, got, views, here)
     recv = exchange(answers)
-    image, returned = render(recv, owner, rank, inverse, target.reshape(tiles, 3, PIX))
+    image, returned = render(recv, owner, rank, target.reshape(tiles, 3, PIX))
     given = exchange(returned)
     d_centres, d_shape, d_logit, d_colours = back(
         centres, shape_raw, logit, colours, flat_camera, got, given, views, here

time: 178 us -> 117 us (0.66)
  Pallas kernels: 111 us -> 50.1 us
    pallas_call x1, Pallas kernels: 86.5 us -> 34.7 us  [render(): pl.pallas_call(render_kernel, out_shape=(shape(target.shape), shape(recv....]
    pallas_call x1, Pallas kernels: 14.3 us -> 5.27 us  [route(): pl.pallas_call(partial(route_kernel, own_count), out_shape=(shape((device...]
  transfers between devices with their start and end apart: 3 -> 3, of which waited for: 3 -> 3; matrix products, arithmetic and copies ran while one was open for 1% -> 2% of each run, Pallas kernels for 0% -> 0%
where the time goes in v2:
time: 117 us
  Pallas kernels  50.1 us (43%)
  waiting for transfers between devices  36.4 us (31%)
  starting transfers between devices  20.2 us (17%)
  local copies, waits for them, and re-layouts  6.95 us (6%)
  other arithmetic  2.42 us (2%)
    pallas_call x1, Pallas kernels, render(): pl.pallas_call(render_kernel, out_shape=(shape(target.shape), shape(recv....  34.7 us
    all_to_all x1, waiting for transfers between devices, shards(): recv = exchange(answers)  14.1 us
    all_to_all x1, waiting for transfers between devices, shards(): given = exchange(returned)  12.5 us
    all_to_all x1, starting transfers between devices, shards(): got = exchange(jnp.concatenate([send, told], axis=1))  11.5 us
    all_to_all x1, waiting for transfers between devices, shards(): got = exchange(jnp.concatenate([send, told], axis=1))  9.79 us
    pallas_call x1, Pallas kernels, back(): pl.pallas_call(partial(back_kernel, views, here), out_shape=(shape(centre...  6.42 us
    pallas_call x1, Pallas kernels, route(): pl.pallas_call(partial(route_kernel, own_count), out_shape=(shape((device...  5.27 us
    all_to_all x1, starting transfers between devices, shards(): given = exchange(returned)  4.63 us
  transfers between devices with their start and end apart: 3, of which 3 were waited for; matrix products, arithmetic and copies ran while one was open for 2% of the time, Pallas kernels for 0%

profile of v2, /device:TPU:1, one launch (start us, length us, event | category | flops | bytes accessed | tf_op | source)
XLA Modules:
  0.0 116.9 jit_solution(244637269866462240)
XLA Ops:
  0.6 0.0 copy-start.7
  0.6 0.6 compare_reduce_fusion
  1.3 0.0 copy-done.7
  1.3 0.1 reshape.152.live_ref
  1.4 0.1 reduce_sum.36
  1.5 0.7 broadcast_select_fusion
  2.2 0.0 copy-start.3
  2.2 0.7 copy-done.3
  3.0 0.0 copy-start.4
  3.0 0.8 copy-done.4
  3.7 5.3 %route.1 = (s32[128,128]{1,0:T(8,128)S(1)}, s32[32,1,256]{2,1,0:T(1,128)S(1)}, s32[32,1,256]{2,1,0:T(1,128)S(1)}) custom-call(s32[32,256]{1,0:T(8,128)S(1)} %bitcast.28, s32[32,256]{1,0:T(8,128)S(1)} %bitcast.29, s32[32,1]{1,0:T(8,128)S(1)} %reshape.152.live_ref), custom_call_target="tpu_custom_call" | custom-call | tf_op jit(solution)/shard_map/route/pallas_call | solution.py:368
  9.0 0.8 copy.32
  9.8 0.0 copy-start.8
  9.8 11.5 %all-to-all-start = ((s32[128,1,256]{2,1,0:T(1,128)}), s32[128,1,256]{2,1,0:T(1,128)S(1)}, u32[]{:S(2)}, u32[]{:S(2)}) async-start(s32[128,1,256]{2,1,0:T(1,128)} %copy.32), calls=%async_computation | async-start | bytes 262144 | tf_op jit(solution)/shard_map/all_to_all | solution.py:448
  21.3 0.0 copy-done.8
  21.3 0.1 copy.30
  21.4 0.1 reshape.145.camera_ref
  21.5 0.0 copy-start
  21.5 0.0 copy-start.1
  21.5 0.0 copy-start.2
  21.5 9.8 %all-to-all-done = s32[128,1,256]{2,1,0:T(1,128)S(1)} async-done(((s32[128,1,256]{2,1,0:T(1,128)}), s32[128,1,256]{2,1,0:T(1,128)S(1)}, u32[]{:S(2)}, u32[]{:S(2)}) %all-to-all-start) | async-done | bytes 131104 | tf_op jit(solution)/shard_map/all_to_all | solution.py:448
  31.3 0.0 copy-start.5
  31.3 0.0 copy-done
  31.3 0.0 copy-done.1
  31.3 0.0 copy-done.2
  31.4 0.6 copy-done.5
  32.0 3.7 %answer.1 = f32[128,1152]{1,0:T(8,128)S(1)} custom-call(f32[3,1024]{1,0:T(4,128)S(1)} %copy-done.1, f32[6,1024]{1,0:T(8,128)S(1)} %copy-done, f32[8,128]{1,0:T(8,128)S(1)} %bitcast.30, f32[3,1024]{1,0:T(4,128)S(1)} %copy-done.2, f32[64]{0:T(128)S(1)} %reshape.145.camera_ref, s32[128,256]{1,0:T(8,128)S(1)} %bitcast.22), custom_call_target="tpu_custom_call" | custom-call | tf_op jit(solution)/shard_map/answer/pallas_call | solution.py:380
  35.7 1.4 %copy.33 = f32[128,1,1152]{2,1,0:T(1,128)} copy(f32[128,1,1152]{2,0,1:T(8,128)S(1)} %bitcast.21) | data formatting | bytes 1179648 | tf_op jit(solution)/shard_map/all_to_all | solution.py:452
  37.1 0.0 copy-start.6
  37.1 4.1 %all-to-all-start.1 = ((f32[128,1,1152]{2,1,0:T(1,128)}), f32[128,1,1152]{2,1,0:T(1,128)S(1)}, u32[]{:S(2)}, u32[]{:S(2)}) async-start(f32[128,1,1152]{2,1,0:T(1,128)} %copy.33), calls=%async_computation.1 | async-start | bytes 1179648 | tf_op jit(solution)/shard_map/all_to_all | solution.py:452
  41.2 0.0 copy-done.6
  41.2 0.1 copy.34
  41.3 14.1 %all-to-all-done.1 = f32[128,1,1152]{2,1,0:T(1,128)S(1)} async-done(((f32[128,1,1152]{2,1,0:T(1,128)}), f32[128,1,1152]{2,1,0:T(1,128)S(1)}, u32[]{:S(2)}, u32[]{:S(2)}) %all-to-all-start.1) | async-done | bytes 589856 | tf_op jit(solution)/shard_map/all_to_all | solution.py:452
  55.4 34.7 %render.1 = (f32[32,3,256]{2,1,0:T(4,128)S(1)}, f32[128,1152]{1,0:T(8,128)S(1)}) custom-call(f32[128,1152]{1,0:T(8,128)S(1)} %bitcast.19, s32[32,1,256]{2,1,0:T(1,128)S(1)} %get-tuple-element.28.owner_ref, s32[32,1,256]{2,1,0:T(1,128)S(1)} %get-tuple-element.29.rank_ref, f32[32,3,256]{2,1,0:T(4,128)S(1)} %bitcast.26), custom_call_target="tpu_custom_call" | custom-call | tf_op jit(solution)/shard_map/render/pallas_call | solution.py:396
  90.2 1.4 %copy.35 = f32[128,1,1152]{2,1,0:T(1,128)} copy(f32[128,1,1152]{2,0,1:T(8,128)S(1)} %bitcast.25) | data formatting | bytes 1179648 | tf_op jit(solution)/shard_map/all_to_all | solution.py:454
  91.6 4.6 %all-to-all-start.2 = ((f32[128,1,1152]{2,1,0:T(1,128)}), f32[128,1,1152]{2,1,0:T(1,128)S(1)}, u32[]{:S(2)}, u32[]{:S(2)}) async-start(f32[128,1,1152]{2,1,0:T(1,128)} %copy.35), calls=%async_computation.2 | async-start | bytes 1179648 | tf_op jit(solution)/shard_map/all_to_all | solution.py:454
  96.3 0.1 select_reduce_fusion.2
  96.4 0.1 select_reduce_fusion.1
  96.5 0.8 and_select_fusion
  97.2 0.7 copy.36
  97.9 12.5 %all-to-all-done.2 = f32[128,1,1152]{2,1,0:T(1,128)S(1)} async-done(((f32[128,1,1152]{2,1,0:T(1,128)}), f32[128,1,1152]{2,1,0:T(1,128)S(1)}, u32[]{:S(2)}, u32[]{:S(2)}) %all-to-all-start.2) | async-done | bytes 589856 | tf_op jit(solution)/shard_map/all_to_all | solution.py:454
  110.5 6.4 %back.1 = (f32[3,1024]{1,0:T(4,128)}, f32[6,1024]{1,0:T(8,128)}, f32[8,128]{1,0:T(8,128)}, f32[3,1024]{1,0:T(4,128)}) custom-call(f32[3,1024]{1,0:T(4,128)S(1)} %copy-done.1, f32[6,1024]{1,0:T(8,128)S(1)} %copy-done, f32[8,128]{1,0:T(8,128)S(1)} %bitcast.31, f32[3,1024]{1,0:T(4,128)S(1)} %copy-done.2, f32[64]{0:T(128)S(1)} %reshape.145.camera_ref, ...), custom_call_target="tpu_custom_call" | custom-call | tf_op jit(solution)/shard_map/back/pallas_call | solution.py:415
  (8 shorter events, 0.1 us)
Async XLA Ops:
  0.6 0.7 copy-start.7
  2.2 0.8 copy-start.3
  3.0 0.8 copy-start.4
  9.8 11.5 %copy-start.8 = (f32[8,2,4]{0,2,1:T(4,128)S(1)}, f32[8,2,4]{0,2,1:T(4,128)}, u32[]{:S(2)}) copy-start(f32[8,2,4]{0,2,1:T(4,128)} %param.15) | copy-start | bytes 772
  9.8 21.5 %all-to-all-start = ((s32[128,1,256]{2,1,0:T(1,128)}), s32[128,1,256]{2,1,0:T(1,128)S(1)}, u32[]{:S(2)}, u32[]{:S(2)}) async-start(s32[128,1,256]{2,1,0:T(1,128)} %copy.32), calls=%async_computation | async-start | bytes 262144 | tf_op jit(solution)/shard_map/all_to_all | solution.py:448
  21.5 9.8 %copy-start = (f32[6,1024]{1,0:T(8,128)S(1)}, f32[6,1024]{1,0:T(8,128)}, u32[]{:S(2)}) copy-start(f32[6,1024]{1,0:T(8,128)} %shape_ref.3) | copy-start | bytes 73732
  21.5 9.8 %copy-start.1 = (f32[3,1024]{1,0:T(4,128)S(1)}, f32[3,1024]{1,0:T(4,128)}, u32[]{:S(2)}) copy-start(f32[3,1024]{1,0:T(4,128)} %centres_ref.3) | copy-start | bytes 36868
  21.5 9.8 %copy-start.2 = (f32[3,1024]{1,0:T(4,128)S(1)}, f32[3,1024]{1,0:T(4,128)}, u32[]{:S(2)}) copy-start(f32[3,1024]{1,0:T(4,128)} %colours_ref.3) | copy-start | bytes 36868
  31.3 0.7 copy-start.5
  37.1 4.1 %copy-start.6 = (f32[2,16,3,256]{3,1,2,0:T(8,128)S(1)}, f32[2,16,3,256]{3,1,2,0:T(8,128)}, u32[]{:S(2)}) copy-start(f32[2,16,3,256]{3,1,2,0:T(8,128)} %param.16) | copy-start | bytes 294916
  37.1 18.3 %all-to-all-start.1 = ((f32[128,1,1152]{2,1,0:T(1,128)}), f32[128,1,1152]{2,1,0:T(1,128)S(1)}, u32[]{:S(2)}, u32[]{:S(2)}) async-start(f32[128,1,1152]{2,1,0:T(1,128)} %copy.33), calls=%async_computation.1 | async-start | bytes 1179648 | tf_op jit(solution)/shard_map/all_to_all | solution.py:452
  91.6 18.8 %all-to-all-start.2 = ((f32[128,1,1152]{2,1,0:T(1,128)}), f32[128,1,1152]{2,1,0:T(1,128)S(1)}, u32[]{:S(2)}, u32[]{:S(2)}) async-start(f32[128,1,1152]{2,1,0:T(1,128)} %copy.35), calls=%async_computation.2 | async-start | bytes 1179648 | tf_op jit(solution)/shard_map/all_to_all | solution.py:454

commit v3 on v2

--- a/solution.py
+++ b/solution.py
@@ -49,33 +49,90 @@
     return lax.dot_general(a, b, (((0,), (0,)), ((), ())), preferred_element_type=F32)
 
 
-def route_kernel(own_count, ids_ref, order_ref, live_ref, send_ref, owner_ref, rank_ref, value_ref, acc_ref):
+MESH = pl.DeviceIdType.MESH
+
+
+class Ring:
+    def __init__(self, view_group, tile_group):
+        self.bits = tile_group.bit_length() - 1
+        self.tiles = tile_group
+        self.count = view_group * tile_group
+        self.me = lax.axis_index("view") * tile_group + lax.axis_index("tile")
+
+    def place(self, device):
+        return (device >> self.bits, device & (self.tiles - 1))
+
+    def after(self, step):
+        return (self.me + step) & (self.count - 1)
+
+    def greet(self, step):
+        pl.semaphore_signal(
+            pltpu.get_barrier_semaphore(), inc=1, device_id=self.place(self.after(step)), device_id_type=MESH
+        )
+
+    def copy(self, source, target, send_sem, recv_sem, device):
+        return pltpu.make_async_remote_copy(
+            src_ref=source,
+            dst_ref=target,
+            send_sem=send_sem.at[device],
+            recv_sem=recv_sem.at[self.me],
+            device_id=self.place(device),
+            device_id_type=MESH,
+        )
+
+
+def each(first, last, unroll, body):
+    def step(n, carry):
+        body(n)
+        return carry
+
+    lax.fori_loop(first, last, step, 0, unroll=unroll)
+
+
+def ask_kernel(
+    sizes, views, ids_ref, order_ref, live_ref, centres_ref, shape_ref, logit_ref, colours_ref, camera_ref,
+    recv_ref, got_ref, owner_ref, rank_ref,
+    value_ref, acc_ref, send_ref, answer_ref, moving_ref, fixed_ref,
+    request_send, request_recv, answer_send, answer_recv, local_sem,
+):
+    ring = Ring(*sizes)
+    me, devices = ring.me, ring.count
     tiles, slots = ids_ref.shape
+    here, tiles_here = live_ref.shape
+    own_count = centres_ref.shape[1]
     own_bits = own_count.bit_length() - 1
-    devices = acc_ref.shape[0] // 2
     blocks = slots // LANES
-    local_view = (iota((tiles, LANES), 0) >= tiles // 2).astype(I32)
+    per_tile = devices // tiles
+    turned = live_ref[...].astype(F32).T
+    live = jnp.concatenate([turned[:, n : n + 1] for n in range(here)], axis=0).astype(I32)
+    local_view = (iota((tiles, LANES), 0) >= tiles_here).astype(I32)
     for block in range(blocks):
-        here = slice(block * LANES, (block + 1) * LANES)
-        order = order_ref[:, here]
+        cut = slice(block * LANES, (block + 1) * LANES)
+        order = order_ref[:, cut]
         low, high = order & (LANES - 1), order >> LANE_BITS
         picked = jnp.zeros((tiles, LANES), I32)
         for source in range(blocks):
             found = lanes(ids_ref[:, source * LANES : (source + 1) * LANES], low)
             picked = jnp.where(high == source, found, picked)
-        owner = jnp.where(order < live_ref[...], picked >> own_bits, -1)
+        owner = jnp.where(order < live, picked >> own_bits, -1)
         value = (picked & (own_count - 1)) + local_view * own_count
         for t in range(tiles):
-            owner_ref[t, :, here] = owner[t : t + 1, :]
-            value_ref[t, :, here] = value[t : t + 1, :]
+            owner_ref[t, :, cut] = owner[t : t + 1, :]
+            value_ref[t, :, cut] = value[t : t + 1, :]
     upto = (iota((slots, slots), 0) <= iota((slots, slots), 1)).astype(BF16)
     acc_ref[...] = jnp.zeros_like(acc_ref)
     peers = iota((devices, slots), 0)
     ranks = iota((LANES, slots), 0)
 
     def tile(t, before):
-        owner = owner_ref[t]
-        value = value_ref[t]
+        for n in range(per_tile - 1):
+            ring.greet(t * per_tile + n + 1)
+
+        @pl.when(t < tiles - 1)
+        def _():
+            ring.greet(t * per_tile + per_tile)
+
+        owner, value = owner_ref[t], value_ref[t]
         named = peers == owner
         count = dot_nn(named.astype(BF16), upto)
         rank = jnp.sum(jnp.where(named, count + before, 0.0), axis=0, keepdims=True) - 1.0
@@ -89,7 +146,81 @@
 
     lax.fori_loop(0, tiles, tile, jnp.zeros((devices, 1), F32), unroll=8)
     low, high = acc_ref[0:devices, :].astype(I32), acc_ref[devices:, :].astype(I32)
-    send_ref[...] = low + 256 * high
+    lane = iota((1, LANES), 1)
+    told = jnp.zeros((1, LANES), I32)
+    for n in range(here):
+        total = jnp.sum(live[n * tiles_here : (n + 1) * tiles_here].astype(F32), axis=0, keepdims=True)
+        told = jnp.where(lane == n, total.astype(I32), told)
+    send_ref[:, 0, 0:LANES] = low + 256 * high
+    send_ref[:, 0, LANES:] = spread(told, devices)
+
+    pl.semaphore_wait(pltpu.get_barrier_semaphore(), devices - 1)
+    own_request = pltpu.make_async_copy(send_ref.at[me], got_ref.at[me], local_sem.at[0])
+    own_request.start()
+
+    def request(device):
+        return ring.copy(send_ref.at[device], got_ref.at[me], request_send, request_recv, device)
+
+    each(1, devices, 16, lambda step: request(ring.after(step)).start())
+
+    centres = [field_of(centres_ref, n) for n in range(3)]
+    shape_raw = [field_of(shape_ref, n) for n in range(6)]
+    for view in range(views):
+        found = moving_fields(centres, shape_raw, camera_view(camera_ref, view))
+        for k in range(MOVING):
+            moving_ref[view // here, k, (view % here) * ROWS : (view % here + 1) * ROWS, :] = found[k]
+    fixed_ref[0] = opacity_of(logit_ref[...])
+    for n in range(3):
+        fixed_ref[1 + n] = field_of(colours_ref, n)
+    own_request.wait()
+    steps = devices // ROWS
+    per_group = steps // (views // here)
+
+    def arrived(semaphores, target, device):
+        pltpu.make_async_copy(target, target, semaphores.at[device]).wait()
+
+    def answer(device):
+        return ring.copy(answer_ref.at[:, device], recv_ref.at[:, me], answer_send, answer_recv, device)
+
+    def block(n):
+        turn = ((me >> 3) - n) & (steps - 1)
+        row = pl.multiple_of(turn * ROWS, ROWS)
+        group = turn // per_group
+        for s in range(ROWS):
+
+            @pl.when(row + s != me)
+            def _(s=s):
+                arrived(request_recv, got_ref.at[row + s], row + s)
+
+        ids = got_ref[pl.ds(row, ROWS), 0, 0:LANES]
+        low, high = ids & (LANES - 1), ids >> LANE_BITS
+        high_fixed = high & (ROWS - 1)
+        for k in range(FIELDS):
+            moves = k < MOVING
+            total = jnp.zeros((ROWS, LANES), F32)
+            for h in range(ROWS * here if moves else ROWS):
+                line = moving_ref[group, k, h : h + 1, :] if moves else fixed_ref[k - MOVING, h : h + 1, :]
+                total = jnp.where((high if moves else high_fixed) == h, lanes(spread(line, ROWS), low), total)
+            answer_ref[k, pl.ds(row, ROWS), 0, :] = total
+        for s in range(ROWS):
+            device = row + ((me + s) & (ROWS - 1))
+
+            @pl.when(device != me)
+            def _(device=device):
+                answer(device).start()
+
+    each(0, steps, 1, block)
+    own_answer = pltpu.make_async_copy(answer_ref.at[:, me], recv_ref.at[:, me], local_sem.at[1])
+    own_answer.start()
+
+    def finish(step):
+        device = ring.after(step)
+        request(device).wait_send()
+        answer(device).wait_send()
+        arrived(answer_recv, recv_ref.at[:, device], device)
+
+    each(1, devices, 16, finish)
+    own_answer.wait()
 
 
 def field_of(ref, row):
@@ -122,56 +253,46 @@
 
 
 def camera_view(camera_ref, view):
-    return [camera_ref[view * 8 + n] for n in range(8)]
-
-
-def answer_kernel(views, here, centres_ref, shape_ref, logit_ref, colours_ref, camera_ref, got_ref, out_ref, moving_ref, fixed_ref):
-    centres = [field_of(centres_ref, n) for n in range(3)]
-    shape_raw = [field_of(shape_ref, n) for n in range(6)]
-    for view in range(views):
-        found = moving_fields(centres, shape_raw, camera_view(camera_ref, view))
-        for k in range(MOVING):
-            moving_ref[view // here, k, (view % here) * ROWS : (view % here + 1) * ROWS, :] = found[k]
-    fixed_ref[0] = opacity_of(logit_ref[...])
-    for n in range(3):
-        fixed_ref[1 + n] = field_of(colours_ref, n)
-    devices = got_ref.shape[0]
-    per_group = devices // (views // here) // ROWS
-
-    def block(n, carry):
-        row = pl.multiple_of(n * ROWS, ROWS)
-        group = n // per_group
-        ids = got_ref[pl.ds(row, ROWS), 0:LANES]
-        low, high = ids & (LANES - 1), ids >> LANE_BITS
-        high_fixed = high & (ROWS - 1)
-        for k in range(FIELDS):
-            moves = k < MOVING
-            total = jnp.zeros((ROWS, LANES), F32)
-            for h in range(ROWS * here if moves else ROWS):
-                line = moving_ref[group, k, h : h + 1, :] if moves else fixed_ref[k - MOVING, h : h + 1, :]
-                total = jnp.where((high if moves else high_fixed) == h, lanes(spread(line, ROWS), low), total)
-            out_ref[pl.ds(row, ROWS), k * LANES : (k + 1) * LANES] = total
-        return carry
-
-    lax.fori_loop(0, devices // ROWS, block, 0)
-
-
-def back_kernel(
-    views, here, centres_ref, shape_ref, logit_ref, colours_ref, camera_ref, got_ref, given_ref,
-    d_centres_ref, d_shape_ref, d_logit_ref, d_colours_ref, moving_ref, fixed_ref,
+    return [camera_ref[view, n // 4, n % 4] for n in range(8)]
+
+
+def give_kernel(
+    sizes, views, here, centres_ref, shape_ref, logit_ref, colours_ref, camera_ref, got_ref, table_ref,
+    d_centres_ref, d_shape_ref, d_logit_ref, d_colours_ref,
+    given_ref, moving_ref, fixed_ref, send_sem, recv_sem, local_sem,
 ):
-    devices = got_ref.shape[0]
+    ring = Ring(*sizes)
+    me, devices = ring.me, ring.count
+    each(1, devices, 16, ring.greet)
     groups = views // here
     moving_ref[...] = jnp.zeros_like(moving_ref)
     fixed_ref[...] = jnp.zeros_like(fixed_ref)
     wide = ROWS * here
     per_step = 2
-
-    def block(n, carry):
-        row = pl.multiple_of(n * ROWS, ROWS)
-        group = n // (devices // groups // ROWS)
-        ids = got_ref[pl.ds(row, ROWS), 0:LANES]
-        values = [given_ref[pl.ds(row, ROWS), k * LANES : (k + 1) * LANES] for k in range(FIELDS)]
+    own = pltpu.make_async_copy(table_ref.at[:, me], given_ref.at[:, me], local_sem)
+    own.start()
+    pl.semaphore_wait(pltpu.get_barrier_semaphore(), devices - 1)
+
+    def copy(device):
+        return ring.copy(table_ref.at[:, device], given_ref.at[:, me], send_sem, recv_sem, device)
+
+    each(1, devices, 16, lambda step: copy(ring.after(step)).start())
+    own.wait()
+    steps = devices // ROWS
+
+    def block(n):
+        turn = ((me >> 3) - n) & (steps - 1)
+        row = pl.multiple_of(turn * ROWS, ROWS)
+        group = turn // (steps // groups)
+        for s in range(ROWS):
+
+            @pl.when(row + s != me)
+            def _(s=s):
+                target = given_ref.at[:, row + s]
+                pltpu.make_async_copy(target, target, recv_sem.at[row + s]).wait()
+
+        ids = got_ref[pl.ds(row, ROWS), 0, 0:LANES]
+        values = [given_ref[k, pl.ds(row, ROWS), 0, :] for k in range(FIELDS)]
         total = None
         for first in range(0, ROWS, per_step):
             lefts, onehots = [], []
@@ -191,9 +312,9 @@
             total = found if total is None else total + found
         moving_ref[group] += total[: MOVING * wide]
         fixed_ref[...] += total[MOVING * wide :]
-        return carry
-
-    lax.fori_loop(0, devices // ROWS, block, 0)
+
+    each(0, steps, 1, block)
+    each(1, devices, 16, lambda step: copy(ring.after(step)).wait_send())
 
     centres = [field_of(centres_ref, n) for n in range(3)]
     shape_raw = [field_of(shape_ref, n) for n in range(6)]
@@ -223,13 +344,35 @@
     d_logit_ref[...] = pull(fixed_ref[0:ROWS, :])[0]
 
 
+def next_owner(ring, got_ref, live_ref, next_ref):
+    here, tiles_here = live_ref.shape
+    counts = got_ref[:, 0, LANES:].astype(F32)
+    source = iota((ring.count, LANES), 0)
+    mine = source >> ring.bits == lax.axis_index("view")
+    lower = mine & ((source & (ring.tiles - 1)) < lax.axis_index("tile"))
+    own_lane = iota((here, LANES), 0) == iota((here, LANES), 1)
+
+    def column(mask):
+        row = jnp.sum(jnp.where(mask, counts, 0.0), axis=0, keepdims=True)
+        return jnp.sum(jnp.where(own_lane, spread(row, here), 0.0), axis=1, keepdims=True)
+
+    whole, before = column(mine), column(lower)
+    earlier = (iota((tiles_here, tiles_here), 0) < iota((tiles_here, tiles_here), 1)).astype(BF16)
+    start = before + dot_nn(live_ref[...].astype(F32).astype(BF16), earlier)
+    above, below = (start * ring.tiles).astype(I32), whole.astype(I32)
+    quotient = (start * ring.tiles / whole).astype(I32)
+    rest = above - quotient * below
+    next_ref[...] = quotient + (rest >= below).astype(I32) - (rest < 0).astype(I32)
+
+
 def render_kernel(
-    recv_ref, owner_ref, rank_ref, target_ref, image_ref, back_ref,
+    sizes, recv_ref, owner_ref, rank_ref, target_ref, got_ref, live_ref, image_ref, back_ref, next_ref,
     cov_ref, odds_ref, high_ref, low_ref, dots_ref, acc_ref,
 ):
     tiles, _, slots = owner_ref.shape
-    devices = recv_ref.shape[0]
+    devices = recv_ref.shape[1]
     blocks = slots // LANES
+    next_owner(Ring(*sizes), got_ref, live_ref, next_ref)
     half = (SIDE - 1) / 2.0
     log2e = 1.4426950408889634
     before = (iota((slots, slots), 0) < iota((slots, slots), 1)).astype(BF16)
@@ -247,7 +390,7 @@
         for group in range(devices // ROWS):
             mine = owner == group * ROWS
             for k in range(FIELDS):
-                table = recv_ref[group * ROWS : (group + 1) * ROWS, k * LANES : (k + 1) * LANES]
+                table = recv_ref[k, group * ROWS : (group + 1) * ROWS, :]
                 total[k] = jnp.where(mine, lanes(table, rank), total[k])
         return [jnp.sum(one, axis=0, keepdims=True) for one in total]
 
@@ -346,7 +489,7 @@
     lax.fori_loop(0, tiles // TOGETHER, together, 0)
     for k in range(FIELDS):
         for n in range(2):
-            back_ref[n * split : (n + 1) * split, k * LANES : (k + 1) * LANES] = acc_ref[
+            back_ref[k, n * split : (n + 1) * split, :] = acc_ref[
                 k * split : (k + 1) * split, n * LANES : (n + 1) * LANES
             ]
 
@@ -355,123 +498,130 @@
 SMEM = pl.BlockSpec(memory_space=pltpu.SMEM)
 
 
-def params():
-    return pltpu.CompilerParams(vmem_limit_bytes=40 * 2**20)
+def params(number=None):
+    limit = 40 * 2**20
+    if number is None:
+        return pltpu.CompilerParams(vmem_limit_bytes=limit)
+    return pltpu.CompilerParams(vmem_limit_bytes=limit, collective_id=number, has_side_effects=True)
 
 
 def shape(dims, kind=F32):
     return jax.ShapeDtypeStruct(dims, kind)
 
 
-def route(ids, order, live, devices, own_count):
+def dma(*dims):
+    return pltpu.SemaphoreType.DMA(dims)
+
+
+def ask(sizes, ids, order, live, centres, shape_raw, logit, colours, camera):
     tiles, slots = ids.shape
+    devices, views, here = sizes[0] * sizes[1], camera.shape[0], live.shape[0]
+    table = (FIELDS, devices, 1, LANES)
     return pl.pallas_call(
-        partial(route_kernel, own_count),
-        out_shape=(shape((devices, LANES), I32), shape((tiles, 1, slots), I32), shape((tiles, 1, slots), I32)),
-        in_specs=[VMEM] * 3,
-        out_specs=(VMEM,) * 3,
-        scratch_shapes=[pltpu.VMEM((tiles, 1, slots), I32), pltpu.VMEM((2 * devices, LANES), F32)],
-        compiler_params=params(),
-        name="route",
-    )(ids, order, live)
-
-
-def answer(centres, shape_raw, logit, colours, camera, got, views, here):
-    return pl.pallas_call(
-        partial(answer_kernel, views, here),
-        out_shape=shape((got.shape[0], FIELDS * LANES)),
-        in_specs=[VMEM] * 4 + [SMEM, VMEM],
-        out_specs=VMEM,
+        partial(ask_kernel, sizes, views),
+        out_shape=(
+            shape(table),
+            shape((devices, 1, 2 * LANES), I32),
+            shape((tiles, 1, slots), I32),
+            shape((tiles, 1, slots), I32),
+        ),
+        in_specs=[VMEM] * 7 + [SMEM],
+        out_specs=(VMEM,) * 4,
         scratch_shapes=[
+            pltpu.VMEM((tiles, 1, slots), I32),
+            pltpu.VMEM((2 * devices, LANES), F32),
+            pltpu.VMEM((devices, 1, 2 * LANES), I32),
+            pltpu.VMEM(table, F32),
             pltpu.VMEM((views // here, MOVING, here * ROWS, LANES), F32),
             pltpu.VMEM((FIELDS - MOVING, ROWS, LANES), F32),
+            dma(devices),
+            dma(devices),
+            dma(devices),
+            dma(devices),
+            dma(2),
         ],
-        compiler_params=params(),
-        name="answer",
-    )(centres, shape_raw, logit, colours, camera, got)
-
-
-def render(recv, owner, rank, target):
+        compiler_params=params(0),
+        name="ask",
+    )(ids, order, live, centres, shape_raw, logit, colours, camera)
+
+
+def render(sizes, recv, owner, rank, target, got, live):
     tiles, _, slots = owner.shape
     return pl.pallas_call(
-        render_kernel,
-        out_shape=(shape(target.shape), shape(recv.shape)),
-        in_specs=[VMEM] * 4,
-        out_specs=(VMEM, VMEM),
+        partial(render_kernel, sizes),
+        out_shape=(shape(target.shape), shape(recv.shape), shape(live.shape, I32)),
+        in_specs=[VMEM] * 6,
+        out_specs=(VMEM,) * 3,
         scratch_shapes=[
             pltpu.VMEM((TOGETHER, PIX, slots), F32),
             pltpu.VMEM((TOGETHER, PIX, slots), F32),
             pltpu.VMEM((TOGETHER, PIX, slots), BF16),
             pltpu.VMEM((TOGETHER, PIX, slots), BF16),
             pltpu.VMEM((TOGETHER, PIX, slots), F32),
-            pltpu.VMEM((FIELDS * recv.shape[0] // 2, 2 * LANES), F32),
+            pltpu.VMEM((FIELDS * recv.shape[1] // 2, 2 * LANES), F32),
         ],
         compiler_params=params(),
         name="render",
-    )(recv, owner, rank, target)
-
-
-def back(centres, shape_raw, logit, colours, camera, got, given, views, here):
+    )(recv, owner, rank, target, got, live)
+
+
+def give(sizes, here, centres, shape_raw, logit, colours, camera, got, table):
+    views = camera.shape[0]
+    devices = got.shape[0]
     return pl.pallas_call(
-        partial(back_kernel, views, here),
+        partial(give_kernel, sizes, views, here),
         out_shape=(shape(centres.shape), shape(shape_raw.shape), shape(logit.shape), shape(colours.shape)),
         in_specs=[VMEM] * 4 + [SMEM, VMEM, VMEM],
         out_specs=(VMEM,) * 4,
         scratch_shapes=[
+            pltpu.VMEM(table.shape, F32),
             pltpu.VMEM((views // here, MOVING * here * ROWS, LANES), F32),
             pltpu.VMEM(((FIELDS - MOVING) * ROWS, LANES), F32),
+            dma(devices),
+            dma(devices),
+            pltpu.SemaphoreType.DMA,
         ],
-        compiler_params=params(),
-        name="back",
-    )(centres, shape_raw, logit, colours, camera, got, given)
+        compiler_params=params(1),
+        name="give",
+    )(centres, shape_raw, logit, colours, camera, got, table)
 
 
 def shards(centres, shape_raw, opacity_logit, colours, camera, target, intersection_ids, depth_order, live_count):
-    view_group, tile_group = lax.axis_size("view"), lax.axis_size("tile")
-    devices = view_group * tile_group
-    own_count = centres.shape[1]
+    sizes = (lax.axis_size("view"), lax.axis_size("tile"))
+    devices = sizes[0] * sizes[1]
     here, tiles_here, slots = intersection_ids.shape
-    views = camera.shape[0]
     tiles = here * tiles_here
-    axes = ("view", "tile")
-    exchange = partial(lax.all_to_all, axis_name=axes, split_axis=0, concat_axis=0, tiled=True)
-
-    send, owner, rank = route(
+    logit = opacity_logit.reshape(ROWS, LANES)
+    recv, got, owner, rank = ask(
+        sizes,
         intersection_ids.reshape(tiles, slots),
         depth_order.reshape(tiles, slots),
-        live_count.reshape(tiles, 1),
-        devices,
-        own_count,
+        live_count,
+        centres,
+        shape_raw,
+        logit,
+        colours,
+        camera,
     )
-    totals = jnp.sum(live_count, axis=1)
-    told = jnp.zeros((devices, LANES), I32).at[:, 0:here].set(totals[None, :])
-    got = exchange(jnp.concatenate([send, told], axis=1))
-    logit = opacity_logit.reshape(ROWS, LANES)
-    flat_camera = camera.reshape(-1)
-    answers = answer(centres, shape_raw, logit, colours, flat_camera, got, views, here)
-    recv = exchange(answers)
-    image, returned = render(recv, owner, rank, target.reshape(tiles, 3, PIX))
-    given = exchange(returned)
-    d_centres, d_shape, d_logit, d_colours = back(
-        centres, shape_raw, logit, colours, flat_camera, got, given, views, here
+    image, table, owners = render(
+        sizes,
+        recv.reshape(FIELDS, devices, LANES),
+        owner,
+        rank,
+        target.reshape(tiles, 3, PIX),
+        got,
+        live_count,
     )
-
-    me_view, me_tile = lax.axis_index("view"), lax.axis_index("tile")
-    source = jnp.arange(devices, dtype=I32)[:, None]
-    in_group = source // tile_group == me_view
-    counts = got[:, LANES : LANES + here]
-    whole = jnp.sum(jnp.where(in_group, counts, 0), axis=0)
-    before = jnp.sum(jnp.where(in_group & (source % tile_group < me_tile), counts, 0), axis=0)
-    earlier = jnp.arange(tiles_here)[:, None] < jnp.arange(tiles_here)[None, :]
-    within = jnp.sum(jnp.where(earlier[None], live_count[:, :, None], 0), axis=1)
-    next_owner = (before[:, None] + within) * tile_group // whole[:, None]
+    d_centres, d_shape, d_logit, d_colours = give(
+        sizes, here, centres, shape_raw, logit, colours, camera, got, table.reshape(FIELDS, devices, 1, LANES)
+    )
     return (
         image.reshape(target.shape),
         d_centres,
         d_shape,
         d_logit.reshape(opacity_logit.shape),
         d_colours,
-        next_owner.astype(I32),
+        owners,
     )
 
 

time: 117 us -> 106 us (0.906)
  Pallas kernels: 50.1 us -> 99.1 us
  waiting for transfers between devices: 36.4 us -> 0 us
  starting transfers between devices: 20.2 us -> 0 us
  other arithmetic: 2.42 us -> 0 us
  local copies, waits for them, and re-layouts: 6.95 us -> 5.52 us
    pallas_call x4 -> x3, Pallas kernels: 50.1 us -> 99.1 us  [the longest x1 42.8 us: ask(): pl.pallas_call(partial(ask_kernel, sizes, views), out_shape=(shape(table)...]
    all_to_all x3 -> x0, waiting for transfers between devices: 36.4 us -> none  [the longest x1 14.1 us: shards(): recv = exchange(answers)]
    all_to_all x3 -> x0, starting transfers between devices: 20.2 us -> none  [the longest x1 11.5 us: shards(): got = exchange(jnp.concatenate([send, told], axis=1))]
    all_to_all x3 -> x0, local copies, waits for them, and re-layouts: 3.64 us -> none  [the longest x1 1.43 us: shards(): recv = exchange(answers)]
    unnamed x24 -> x23, local copies, waits for them, and re-layouts: 3.12 us -> 5.52 us
    another operation x2 -> x0, other arithmetic: 1.3 us -> none
  transfers between devices with their start and end apart: 3 -> 0, of which waited for: 3 -> 0; matrix products, arithmetic and copies ran while one was open for 2% -> 0% of each run, Pallas kernels for 0% -> 0%
where the time goes in v3:
time: 106 us; the launch traced here: 105 us
  Pallas kernels  99.1 us (93%)
  local copies, waits for them, and re-layouts  5.52 us (5%)
    pallas_call x1, Pallas kernels, ask(): pl.pallas_call(partial(ask_kernel, sizes, views), out_shape=(shape(table)...  42.8 us
    pallas_call x1, Pallas kernels, render(): pl.pallas_call(partial(render_kernel, sizes), out_shape=(shape(target.sha...  35.1 us
    pallas_call x1, Pallas kernels, give(): pl.pallas_call(partial(give_kernel, sizes, views, here), out_shape=(shape...  21.1 us
    unnamed x23, local copies, waits for them, and re-layouts  5.52 us

profile of v3, /device:TPU:1, one launch (start us, length us, event | category | flops | bytes accessed | tf_op | source)
XLA Modules:
  0.0 105.4 jit_solution(11431423227380688628)
XLA Ops:
  0.6 0.0 copy-start.7
  0.6 0.7 copy-done.7
  1.3 0.1 copy.15.camera_ref
  1.4 0.0 copy-start
  1.4 0.0 copy-start.1
  1.4 0.0 copy-start.2
  1.4 0.0 copy-start.3
  1.4 0.0 copy-start.4
  1.4 0.0 copy-start.5
  1.4 1.0 copy.16
  2.5 0.0 copy-start.6
  2.5 0.0 copy-done
  2.5 0.0 copy-done.1
  2.5 0.0 copy-done.2
  2.5 0.0 copy-done.3
  2.5 0.0 copy-done.4
  2.5 0.0 copy-done.5
  2.5 0.6 copy-done.6
  3.2 42.8 %ask.1 = (f32[9,128,1,128]{3,2,1,0:T(1,128)S(1)}, s32[128,1,256]{2,1,0:T(1,128)S(1)}, s32[32,1,256]{2,1,0:T(1,128)S(1)}, s32[32,1,256]{2,1,0:T(1,128)S(1)}) custom-call(s32[32,256]{1,0:T(8,128)S(1)} %bitcast.12, s32[32,256]{1,0:T(8,128)S(1)} %bitcast.13, s32[2,16]{1,0:T(2,128)S(1)} %copy-done.6, f32[3,1024]{1,0:T(4,128)S(1)} %copy-done.1, ...), custom_call_target="tpu_custom_call" | custom-call | tf_op jit(solution)/shard_map/ask/pallas_call | solution.py:520
  46.0 35.1 %render.1 = (f32[32,3,256]{2,1,0:T(4,128)S(1)}, f32[9,128,128]{2,1,0:T(8,128)S(1)}, s32[2,16]{1,0:T(2,128)}) custom-call(f32[9,128,128]{2,1,0:T(8,128)S(1)} %bitcast.9, s32[32,1,256]{2,1,0:T(1,128)S(1)} %get-tuple-element.18.owner_ref, s32[32,1,256]{2,1,0:T(1,128)S(1)} %get-tuple-element.19.rank_ref, f32[32,3,256]{2,1,0:T(4,128)S(1)} %bitcast.10, ...), custom_call_target="tpu_custom_call" | custom-call | tf_op jit(solution)/shard_map/render/pallas_call | solution.py:550
  81.1 0.7 copy.18
  81.8 21.1 %give.1 = (f32[3,1024]{1,0:T(4,128)S(1)}, f32[6,1024]{1,0:T(8,128)S(1)}, f32[8,128]{1,0:T(8,128)S(1)}, f32[3,1024]{1,0:T(4,128)S(1)}) custom-call(f32[3,1024]{1,0:T(4,128)S(1)} %copy-done.1, f32[6,1024]{1,0:T(8,128)S(1)} %copy-done, f32[8,128]{1,0:T(8,128)S(1)} %bitcast.15, f32[3,1024]{1,0:T(4,128)S(1)} %copy-done.2, f32[8,2,4]{2,1,0:T(2,128)S(1)} %copy.15.camera_ref, ...), custom_call_target="tpu_custom_call" | custom-call | tf_op jit(solution)/shard_map/give/pallas_call | solution.py:571
  103.0 0.6 copy.23
  103.6 0.6 copy.24
  104.2 0.6 copy.25
  104.8 0.6 copy.26
Async XLA Ops:
  0.6 0.7 copy-start.7
  1.4 1.1 %copy-start = (f32[6,1024]{1,0:T(8,128)S(1)}, f32[6,1024]{1,0:T(8,128)}, u32[]{:S(2)}) copy-start(f32[6,1024]{1,0:T(8,128)} %shape_ref.3) | copy-start | bytes 73732
  1.4 1.1 %copy-start.1 = (f32[3,1024]{1,0:T(4,128)S(1)}, f32[3,1024]{1,0:T(4,128)}, u32[]{:S(2)}) copy-start(f32[3,1024]{1,0:T(4,128)} %centres_ref.3) | copy-start | bytes 36868
  1.4 1.1 %copy-start.2 = (f32[3,1024]{1,0:T(4,128)S(1)}, f32[3,1024]{1,0:T(4,128)}, u32[]{:S(2)}) copy-start(f32[3,1024]{1,0:T(4,128)} %colours_ref.3) | copy-start | bytes 36868
  1.4 1.1 %copy-start.3 = (s32[2,16,256]{2,1,0:T(8,128)S(1)}, s32[2,16,256]{2,1,0:T(8,128)}, u32[]{:S(2)}) copy-start(s32[2,16,256]{2,1,0:T(8,128)} %param.15) | copy-start | bytes 98308
  1.4 1.1 %copy-start.4 = (s32[2,16,256]{2,1,0:T(8,128)S(1)}, s32[2,16,256]{2,1,0:T(8,128)}, u32[]{:S(2)}) copy-start(s32[2,16,256]{2,1,0:T(8,128)} %param.16) | copy-start | bytes 98308
  1.4 1.1 %copy-start.5 = (f32[1024]{0:T(1024)S(1)}, f32[1024]{0:T(1024)}, u32[]{:S(2)}) copy-start(f32[1024]{0:T(1024)} %param.11) | copy-start | bytes 12292
  2.5 0.7 copy-start.6

commit v4 on v3

--- a/solution.py
+++ b/solution.py
@@ -89,13 +89,12 @@
     lax.fori_loop(first, last, step, 0, unroll=unroll)
 
 
-def ask_kernel(
-    sizes, views, ids_ref, order_ref, live_ref, centres_ref, shape_ref, logit_ref, colours_ref, camera_ref,
-    recv_ref, got_ref, owner_ref, rank_ref,
-    value_ref, acc_ref, send_ref, answer_ref, moving_ref, fixed_ref,
+def ask(
+    ring, views, ids_ref, order_ref, live_ref, centres_ref, shape_ref, logit_ref, colours_ref, camera_ref,
+    records_ref, got_ref, owner_ref, rank_ref,
+    value_ref, acc_ref, send_ref, answer_ref, recv_ref, moving_ref, fixed_ref,
     request_send, request_recv, answer_send, answer_recv, local_sem,
 ):
-    ring = Ring(*sizes)
     me, devices = ring.me, ring.count
     tiles, slots = ids_ref.shape
     here, tiles_here = live_ref.shape
@@ -213,14 +212,28 @@
     own_answer = pltpu.make_async_copy(answer_ref.at[:, me], recv_ref.at[:, me], local_sem.at[1])
     own_answer.start()
 
-    def finish(step):
+    own_answer.wait()
+
+    def land(n):
+        turn = ((me >> 3) + n) & (steps - 1)
+        row = pl.multiple_of(turn * ROWS, ROWS)
+        for s in range(ROWS):
+
+            @pl.when(row + s != me)
+            def _(s=s):
+                arrived(answer_recv, recv_ref.at[:, row + s], row + s)
+
+        for k in range(FIELDS):
+            records_ref[k, pl.ds(row, ROWS), :] = recv_ref[k, pl.ds(row, ROWS), 0, :]
+
+    each(0, steps, 1, land)
+
+    def sent(step):
         device = ring.after(step)
         request(device).wait_send()
         answer(device).wait_send()
-        arrived(answer_recv, recv_ref.at[:, device], device)
-
-    each(1, devices, 16, finish)
-    own_answer.wait()
+
+    return lambda: each(1, devices, 16, sent)
 
 
 def field_of(ref, row):
@@ -256,14 +269,8 @@
     return [camera_ref[view, n // 4, n % 4] for n in range(8)]
 
 
-def give_kernel(
-    sizes, views, here, centres_ref, shape_ref, logit_ref, colours_ref, camera_ref, got_ref, table_ref,
-    d_centres_ref, d_shape_ref, d_logit_ref, d_colours_ref,
-    given_ref, moving_ref, fixed_ref, send_sem, recv_sem, local_sem,
-):
-    ring = Ring(*sizes)
+def give(ring, views, here, got_ref, table_ref, given_ref, moving_ref, fixed_ref, send_sem, recv_sem, local_sem):
     me, devices = ring.me, ring.count
-    each(1, devices, 16, ring.greet)
     groups = views // here
     moving_ref[...] = jnp.zeros_like(moving_ref)
     fixed_ref[...] = jnp.zeros_like(fixed_ref)
@@ -271,7 +278,6 @@
     per_step = 2
     own = pltpu.make_async_copy(table_ref.at[:, me], given_ref.at[:, me], local_sem)
     own.start()
-    pl.semaphore_wait(pltpu.get_barrier_semaphore(), devices - 1)
 
     def copy(device):
         return ring.copy(table_ref.at[:, device], given_ref.at[:, me], send_sem, recv_sem, device)
@@ -316,6 +322,13 @@
     each(0, steps, 1, block)
     each(1, devices, 16, lambda step: copy(ring.after(step)).wait_send())
 
+
+def pull_kernel(
+    views, here, centres_ref, shape_ref, logit_ref, camera_ref, moving_ref, fixed_ref, owners_ref,
+    d_centres_ref, d_shape_ref, d_logit_ref, d_colours_ref, next_ref,
+):
+    wide = ROWS * here
+    next_ref[...] = owners_ref[...]
     centres = [field_of(centres_ref, n) for n in range(3)]
     shape_raw = [field_of(shape_ref, n) for n in range(6)]
     d_centres = [jnp.zeros((ROWS, LANES), F32)] * 3
@@ -365,14 +378,13 @@
     next_ref[...] = quotient + (rest >= below).astype(I32) - (rest < 0).astype(I32)
 
 
-def render_kernel(
-    sizes, recv_ref, owner_ref, rank_ref, target_ref, got_ref, live_ref, image_ref, back_ref, next_ref,
+def render(
+    ring, recv_ref, owner_ref, rank_ref, target_ref, image_ref, table_ref,
     cov_ref, odds_ref, high_ref, low_ref, dots_ref, acc_ref,
 ):
     tiles, _, slots = owner_ref.shape
-    devices = recv_ref.shape[1]
+    devices = ring.count
     blocks = slots // LANES
-    next_owner(Ring(*sizes), got_ref, live_ref, next_ref)
     half = (SIDE - 1) / 2.0
     log2e = 1.4426950408889634
     before = (iota((slots, slots), 0) < iota((slots, slots), 1)).astype(BF16)
@@ -431,13 +443,9 @@
         image = drawn[0:3] + drawn[3:6]
         image_ref[t] = image
         error = image - target_ref[t]
-        e_high = error.astype(BF16).astype(F32)
-        e_low = error - e_high
-        d_colour = jnp.concatenate([e_high, e_low], axis=0).astype(BF16)
-        d_colour = dot_nn(d_colour, w_high) + dot_nn(d_colour, w_low)
-        d_colour = d_colour[0:3] + d_colour[3:6]
         yield
         column = jnp.concatenate([error, jnp.zeros((ROWS - 3, PIX), F32)], axis=0).T
+        d_colour = [jnp.sum(weights * column[:, n : n + 1], axis=0, keepdims=True) for n in range(3)]
         shade = column[:, 0:1] * red + column[:, 1:2] * green + column[:, 2:3] * blue
         shaded = weights * shade
         s_high, s_low = halves(shaded)
@@ -466,9 +474,7 @@
             -sxy,
             -0.5 * syy,
             jnp.where(opacity > 0.0, s0 / opacity, 0.0),
-            d_colour[0:1],
-            d_colour[1:2],
-            d_colour[2:3],
+            *d_colour,
         ]
         owner, rank = owner_ref[t], rank_ref[t]
         yield
@@ -489,9 +495,35 @@
     lax.fori_loop(0, tiles // TOGETHER, together, 0)
     for k in range(FIELDS):
         for n in range(2):
-            back_ref[k, n * split : (n + 1) * split, :] = acc_ref[
+            table_ref[k, n * split : (n + 1) * split, 0, :] = acc_ref[
                 k * split : (k + 1) * split, n * LANES : (n + 1) * LANES
             ]
+
+
+def splat_kernel(
+    sizes, views, ids_ref, order_ref, live_ref, centres_ref, shape_ref, logit_ref, colours_ref, camera_ref, target_ref,
+    image_ref, moving_ref, fixed_ref, next_ref,
+    records_ref, got_ref, owner_ref, rank_ref, value_ref, ask_acc_ref, send_ref, answer_ref, recv_ref,
+    own_moving_ref, own_fixed_ref, cov_ref, odds_ref, high_ref, low_ref, dots_ref, acc_ref, table_ref, given_ref,
+    request_send, request_recv, answer_send, answer_recv, give_send, give_recv, local_sem,
+):
+    ring = Ring(*sizes)
+    sent = ask(
+        ring, views, ids_ref, order_ref, live_ref, centres_ref, shape_ref, logit_ref, colours_ref, camera_ref,
+        records_ref, got_ref, owner_ref, rank_ref,
+        value_ref, ask_acc_ref, send_ref, answer_ref, recv_ref, own_moving_ref, own_fixed_ref,
+        request_send, request_recv, answer_send, answer_recv, local_sem,
+    )
+    next_owner(ring, got_ref, live_ref, next_ref)
+    render(
+        ring, records_ref, owner_ref, rank_ref, target_ref, image_ref, table_ref,
+        cov_ref, odds_ref, high_ref, low_ref, dots_ref, acc_ref,
+    )
+    give(
+        ring, views, live_ref.shape[0], got_ref, table_ref, given_ref, moving_ref, fixed_ref,
+        give_send, give_recv, local_sem.at[2],
+    )
+    sent()
 
 
 VMEM = pl.BlockSpec(memory_space=pltpu.VMEM)
@@ -513,86 +545,72 @@
     return pltpu.SemaphoreType.DMA(dims)
 
 
-def ask(sizes, ids, order, live, centres, shape_raw, logit, colours, camera):
+def splat(sizes, ids, order, live, centres, shape_raw, logit, colours, camera, target):
     tiles, slots = ids.shape
     devices, views, here = sizes[0] * sizes[1], camera.shape[0], live.shape[0]
     table = (FIELDS, devices, 1, LANES)
+    line = (tiles, 1, slots)
     return pl.pallas_call(
-        partial(ask_kernel, sizes, views),
+        partial(splat_kernel, sizes, views),
         out_shape=(
-            shape(table),
-            shape((devices, 1, 2 * LANES), I32),
-            shape((tiles, 1, slots), I32),
-            shape((tiles, 1, slots), I32),
+            shape(target.shape),
+            shape((views // here, MOVING * here * ROWS, LANES)),
+            shape(((FIELDS - MOVING) * ROWS, LANES)),
+            shape(live.shape, I32),
         ),
-        in_specs=[VMEM] * 7 + [SMEM],
+        in_specs=[VMEM] * 7 + [SMEM, VMEM],
         out_specs=(VMEM,) * 4,
         scratch_shapes=[
-            pltpu.VMEM((tiles, 1, slots), I32),
+            pltpu.VMEM((FIELDS, devices, LANES), F32),
+            pltpu.VMEM((devices, 1, 2 * LANES), I32),
+            pltpu.VMEM(line, I32),
+            pltpu.VMEM(line, I32),
+            pltpu.VMEM(line, I32),
             pltpu.VMEM((2 * devices, LANES), F32),
             pltpu.VMEM((devices, 1, 2 * LANES), I32),
             pltpu.VMEM(table, F32),
+            pltpu.VMEM(table, F32),
             pltpu.VMEM((views // here, MOVING, here * ROWS, LANES), F32),
             pltpu.VMEM((FIELDS - MOVING, ROWS, LANES), F32),
-            dma(devices),
-            dma(devices),
-            dma(devices),
-            dma(devices),
-            dma(2),
-        ],
-        compiler_params=params(0),
-        name="ask",
-    )(ids, order, live, centres, shape_raw, logit, colours, camera)
-
-
-def render(sizes, recv, owner, rank, target, got, live):
-    tiles, _, slots = owner.shape
-    return pl.pallas_call(
-        partial(render_kernel, sizes),
-        out_shape=(shape(target.shape), shape(recv.shape), shape(live.shape, I32)),
-        in_specs=[VMEM] * 6,
-        out_specs=(VMEM,) * 3,
-        scratch_shapes=[
             pltpu.VMEM((TOGETHER, PIX, slots), F32),
             pltpu.VMEM((TOGETHER, PIX, slots), F32),
             pltpu.VMEM((TOGETHER, PIX, slots), BF16),
             pltpu.VMEM((TOGETHER, PIX, slots), BF16),
             pltpu.VMEM((TOGETHER, PIX, slots), F32),
-            pltpu.VMEM((FIELDS * recv.shape[1] // 2, 2 * LANES), F32),
-        ],
+            pltpu.VMEM((FIELDS * devices // 2, 2 * LANES), F32),
+            pltpu.VMEM(table, F32),
+            pltpu.VMEM(table, F32),
+        ]
+        + [dma(devices)] * 6
+        + [dma(3)],
+        compiler_params=params(0),
+        name="splat",
+    )(ids, order, live, centres, shape_raw, logit, colours, camera, target)
+
+
+def pull(here, centres, shape_raw, logit, camera, moving, fixed, owners):
+    return pl.pallas_call(
+        partial(pull_kernel, camera.shape[0], here),
+        out_shape=(
+            shape(centres.shape),
+            shape(shape_raw.shape),
+            shape(logit.shape),
+            shape(centres.shape),
+            shape(owners.shape, I32),
+        ),
+        in_specs=[VMEM] * 3 + [SMEM] + [VMEM] * 3,
+        out_specs=(VMEM,) * 5,
         compiler_params=params(),
-        name="render",
-    )(recv, owner, rank, target, got, live)
-
-
-def give(sizes, here, centres, shape_raw, logit, colours, camera, got, table):
-    views = camera.shape[0]
-    devices = got.shape[0]
-    return pl.pallas_call(
-        partial(give_kernel, sizes, views, here),
-        out_shape=(shape(centres.shape), shape(shape_raw.shape), shape(logit.shape), shape(colours.shape)),
-        in_specs=[VMEM] * 4 + [SMEM, VMEM, VMEM],
-        out_specs=(VMEM,) * 4,
-        scratch_shapes=[
-            pltpu.VMEM(table.shape, F32),
-            pltpu.VMEM((views // here, MOVING * here * ROWS, LANES), F32),
-            pltpu.VMEM(((FIELDS - MOVING) * ROWS, LANES), F32),
-            dma(devices),
-            dma(devices),
-            pltpu.SemaphoreType.DMA,
-        ],
-        compiler_params=params(1),
-        name="give",
-    )(centres, shape_raw, logit, colours, camera, got, table)
+        name="pull",
+    )(centres, shape_raw, logit, camera, moving, fixed, owners)
 
 
 def shards(centres, shape_raw, opacity_logit, colours, camera, target, intersection_ids, depth_order, live_count):
     sizes = (lax.axis_size("view"), lax.axis_size("tile"))
-    devices = sizes[0] * sizes[1]
     here, tiles_here, slots = intersection_ids.shape
     tiles = here * tiles_here
     logit = opacity_logit.reshape(ROWS, LANES)
-    recv, got, owner, rank = ask(
+    image, moving, fixed, owners = splat(
         sizes,
         intersection_ids.reshape(tiles, slots),
         depth_order.reshape(tiles, slots),
@@ -602,18 +620,10 @@
         logit,
         colours,
         camera,
-    )
-    image, table, owners = render(
-        sizes,
-        recv.reshape(FIELDS, devices, LANES),
-        owner,
-        rank,
         target.reshape(tiles, 3, PIX),
-        got,
-        live_count,
-    )
-    d_centres, d_shape, d_logit, d_colours = give(
-        sizes, here, centres, shape_raw, logit, colours, camera, got, table.reshape(FIELDS, devices, 1, LANES)
+    )
+    d_centres, d_shape, d_logit, d_colours, owners = pull(
+        here, centres, shape_raw, logit, camera, moving, fixed, owners
     )
     return (
         image.reshape(target.shape),

time: 106 us -> 97.1 us (0.916)
  Pallas kernels: 99.1 us -> 93.1 us
  local copies, waits for them, and re-layouts: 5.52 us -> 3.1 us
    pallas_call x3 -> x2, Pallas kernels: 99.1 us -> 93.1 us  [the longest x1 91.6 us: splat(): pl.pallas_call(partial(splat_kernel, sizes, views), out_shape=(shape(targ...]
    unnamed x23 -> x19, local copies, waits for them, and re-layouts: 5.52 us -> 3.1 us
where the time goes in v4:
time: 97.1 us; the launch traced here: 96.9 us
  Pallas kernels  93.1 us (96%)
  local copies, waits for them, and re-layouts  3.1 us (3%)
    pallas_call x1, Pallas kernels, splat(): pl.pallas_call(partial(splat_kernel, sizes, views), out_shape=(shape(targ...  91.6 us
    unnamed x19, local copies, waits for them, and re-layouts  3.1 us

profile of v4, /device:TPU:1, one launch (start us, length us, event | category | flops | bytes accessed | tf_op | source)
XLA Modules:
  0.0 96.9 jit_solution(4744066234611735224)
XLA Ops:
  0.6 0.0 copy-start.7
  0.6 0.7 copy-done.7
  1.3 0.1 copy.16.camera_ref
  1.4 0.0 copy-start
  1.4 0.0 copy-start.1
  1.4 0.0 copy-start.2
  1.4 0.0 copy-start.3
  1.4 0.0 copy-start.4
  1.4 0.0 copy-start.5
  1.4 1.0 %copy.15 = f32[2,16,3,256]{3,2,1,0:T(4,128)S(1)} copy(f32[2,16,3,256]{3,1,2,0:T(8,128)} %param.14) | data formatting | bytes 196608 | tf_op args[5]
  2.5 0.0 copy-start.6
  2.5 0.0 copy-done
  2.5 0.0 copy-done.1
  2.5 0.0 copy-done.2
  2.5 0.0 copy-done.3
  2.5 0.0 copy-done.4
  2.5 0.0 copy-done.5
  2.5 0.6 copy-done.6
  3.2 91.6 %splat.1 = (f32[32,3,256]{2,1,0:T(4,128)S(1)}, f32[4,80,128]{2,1,0:T(8,128)S(1)}, f32[32,128]{1,0:T(8,128)S(1)}, s32[2,16]{1,0:T(2,128)S(1)}) custom-call(s32[32,256]{1,0:T(8,128)S(1)} %bitcast.8, s32[32,256]{1,0:T(8,128)S(1)} %bitcast.9, s32[2,16]{1,0:T(2,128)S(1)} %copy-done.6, f32[3,1024]{1,0:T(4,128)S(1)} %copy-done.1, f32[6,1024]{1,0:T(8,128)S(1)} %copy-done, ...), custom_call_target="tpu_custom_call" | custom-call | tf_op jit(solution)/shard_map/splat/pallas_call | solution.py:553
  94.8 0.7 copy.18
  95.5 1.5 %pull.1 = (f32[3,1024]{1,0:T(4,128)}, f32[6,1024]{1,0:T(8,128)}, f32[8,128]{1,0:T(8,128)}, f32[3,1024]{1,0:T(4,128)}, s32[2,16]{1,0:T(2,128)}) custom-call(f32[3,1024]{1,0:T(4,128)S(1)} %copy-done.1, f32[6,1024]{1,0:T(8,128)S(1)} %copy-done, f32[8,128]{1,0:T(8,128)S(1)} %bitcast.11, f32[8,2,4]{2,1,0:T(2,128)S(1)} %copy.16.camera_ref, ...), custom_call_target="tpu_custom_call" | custom-call | tf_op jit(solution)/shard_map/pull/pallas_call | solution.py:592
Async XLA Ops:
  0.6 0.7 copy-start.7
  1.4 1.1 %copy-start = (f32[6,1024]{1,0:T(8,128)S(1)}, f32[6,1024]{1,0:T(8,128)}, u32[]{:S(2)}) copy-start(f32[6,1024]{1,0:T(8,128)} %shape_ref.3) | copy-start | bytes 73732
  1.4 1.1 %copy-start.1 = (f32[3,1024]{1,0:T(4,128)S(1)}, f32[3,1024]{1,0:T(4,128)}, u32[]{:S(2)}) copy-start(f32[3,1024]{1,0:T(4,128)} %centres_ref.3) | copy-start | bytes 36868
  1.4 1.1 %copy-start.2 = (s32[2,16,256]{2,1,0:T(8,128)S(1)}, s32[2,16,256]{2,1,0:T(8,128)}, u32[]{:S(2)}) copy-start(s32[2,16,256]{2,1,0:T(8,128)} %param.15) | copy-start | bytes 98308
  1.4 1.1 %copy-start.3 = (s32[2,16,256]{2,1,0:T(8,128)S(1)}, s32[2,16,256]{2,1,0:T(8,128)}, u32[]{:S(2)}) copy-start(s32[2,16,256]{2,1,0:T(8,128)} %param.16) | copy-start | bytes 98308
  1.4 1.1 %copy-start.4 = (f32[1024]{0:T(1024)S(1)}, f32[1024]{0:T(1024)}, u32[]{:S(2)}) copy-start(f32[1024]{0:T(1024)} %param.11) | copy-start | bytes 12292
  1.4 1.1 %copy-start.5 = (f32[3,1024]{1,0:T(4,128)S(1)}, f32[3,1024]{1,0:T(4,128)}, u32[]{:S(2)}) copy-start(f32[3,1024]{1,0:T(4,128)} %colours_ref.1) | copy-start | bytes 36868
  2.5 0.7 copy-start.6

commit v5 on v4

--- a/solution.py
+++ b/solution.py
@@ -101,7 +101,6 @@
     own_count = centres_ref.shape[1]
     own_bits = own_count.bit_length() - 1
     blocks = slots // LANES
-    per_tile = devices // tiles
     turned = live_ref[...].astype(F32).T
     live = jnp.concatenate([turned[:, n : n + 1] for n in range(here)], axis=0).astype(I32)
     local_view = (iota((tiles, LANES), 0) >= tiles_here).astype(I32)
@@ -124,13 +123,6 @@
     ranks = iota((LANES, slots), 0)
 
     def tile(t, before):
-        for n in range(per_tile - 1):
-            ring.greet(t * per_tile + n + 1)
-
-        @pl.when(t < tiles - 1)
-        def _():
-            ring.greet(t * per_tile + per_tile)
-
         owner, value = owner_ref[t], value_ref[t]
         named = peers == owner
         count = dot_nn(named.astype(BF16), upto)
@@ -143,7 +135,18 @@
         acc_ref[...] += dot_nt(left, at_rank)
         return before + count[:, slots - 1 :]
 
-    lax.fori_loop(0, tiles, tile, jnp.zeros((devices, 1), F32), unroll=8)
+    def some(n, before):
+        for step in range(greets):
+            ring.greet(n * greets + step + 1)
+        for t in range(ROWS):
+            before = tile(n * ROWS + t, before)
+        return before
+
+    rounds = tiles // ROWS
+    greets = (devices - 1) // rounds
+    for step in range(rounds * greets + 1, devices):
+        ring.greet(step)
+    lax.fori_loop(0, rounds, some, jnp.zeros((devices, 1), F32))
     low, high = acc_ref[0:devices, :].astype(I32), acc_ref[devices:, :].astype(I32)
     lane = iota((1, LANES), 1)
     told = jnp.zeros((1, LANES), I32)
@@ -266,7 +269,7 @@
 
 
 def camera_view(camera_ref, view):
-    return [camera_ref[view, n // 4, n % 4] for n in range(8)]
+    return [camera_ref[n // 4, n % 4, view] for n in range(8)]
 
 
 def give(ring, views, here, got_ref, table_ref, given_ref, moving_ref, fixed_ref, send_sem, recv_sem, local_sem):
@@ -415,6 +418,7 @@
             jnp.concatenate([found[block][k] for block in range(blocks)], axis=1) for k in range(FIELDS)
         )
         yield
+        aim = jnp.concatenate([target_ref[t], jnp.zeros((ROWS - 3, PIX), F32)], axis=0).T
         dx = across - u
         scale = -0.5 * log2e
         first = (scale * a) * dx * dx
@@ -436,15 +440,12 @@
         w_high, w_low = halves(weights)
         yield
         colour = jnp.concatenate([red, green, blue], axis=0)
-        c_high = colour.astype(BF16).astype(F32)
-        c_low = colour - c_high
-        pair = jnp.concatenate([c_high, c_low], axis=0).astype(BF16)
-        drawn = dot_nt(pair, w_high) + dot_nt(pair, w_low)
-        image = drawn[0:3] + drawn[3:6]
-        image_ref[t] = image
-        error = image - target_ref[t]
+        colour = jnp.concatenate([colour, jnp.zeros((ROWS - 3, slots), F32)], axis=0)
+        c_high, c_low = halves(colour)
+        drawn = (dot_nt(w_high, c_high) + dot_nt(w_low, c_high)) + (dot_nt(w_high, c_low) + dot_nt(w_low, c_low))
+        column = drawn - aim
+        image_ref[t] = drawn.T[0:3]
         yield
-        column = jnp.concatenate([error, jnp.zeros((ROWS - 3, PIX), F32)], axis=0).T
         d_colour = [jnp.sum(weights * column[:, n : n + 1], axis=0, keepdims=True) for n in range(3)]
         shade = column[:, 0:1] * red + column[:, 1:2] * green + column[:, 2:3] * blue
         shaded = weights * shade
@@ -504,10 +505,14 @@
     sizes, views, ids_ref, order_ref, live_ref, centres_ref, shape_ref, logit_ref, colours_ref, camera_ref, target_ref,
     image_ref, moving_ref, fixed_ref, next_ref,
     records_ref, got_ref, owner_ref, rank_ref, value_ref, ask_acc_ref, send_ref, answer_ref, recv_ref,
-    own_moving_ref, own_fixed_ref, cov_ref, odds_ref, high_ref, low_ref, dots_ref, acc_ref, table_ref, given_ref,
+    own_moving_ref, own_fixed_ref, cov_ref, odds_ref, high_ref, low_ref, dots_ref, acc_ref, table_ref, given_ref, aims_ref, drawn_ref,
     request_send, request_recv, answer_send, answer_recv, give_send, give_recv, local_sem,
 ):
     ring = Ring(*sizes)
+    here, channels, tiles_here, _ = target_ref.shape
+    places = [(v, c, t) for v in range(here) for c in range(channels) for t in range(tiles_here)]
+    for v, c, t in places:
+        aims_ref[v * tiles_here + t, c : c + 1, :] = target_ref[v, c, t : t + 1, :]
     sent = ask(
         ring, views, ids_ref, order_ref, live_ref, centres_ref, shape_ref, logit_ref, colours_ref, camera_ref,
         records_ref, got_ref, owner_ref, rank_ref,
@@ -516,13 +521,15 @@
     )
     next_owner(ring, got_ref, live_ref, next_ref)
     render(
-        ring, records_ref, owner_ref, rank_ref, target_ref, image_ref, table_ref,
+        ring, records_ref, owner_ref, rank_ref, aims_ref, drawn_ref, table_ref,
         cov_ref, odds_ref, high_ref, low_ref, dots_ref, acc_ref,
     )
     give(
         ring, views, live_ref.shape[0], got_ref, table_ref, given_ref, moving_ref, fixed_ref,
         give_send, give_recv, local_sem.at[2],
     )
+    for v, c, t in places:
+        image_ref[v, c, t : t + 1, :] = drawn_ref[v * tiles_here + t, c : c + 1, :]
     sent()
 
 
@@ -547,7 +554,7 @@
 
 def splat(sizes, ids, order, live, centres, shape_raw, logit, colours, camera, target):
     tiles, slots = ids.shape
-    devices, views, here = sizes[0] * sizes[1], camera.shape[0], live.shape[0]
+    devices, views, here = sizes[0] * sizes[1], camera.shape[2], live.shape[0]
     table = (FIELDS, devices, 1, LANES)
     line = (tiles, 1, slots)
     return pl.pallas_call(
@@ -580,6 +587,8 @@
             pltpu.VMEM((FIELDS * devices // 2, 2 * LANES), F32),
             pltpu.VMEM(table, F32),
             pltpu.VMEM(table, F32),
+            pltpu.VMEM((tiles, 3, PIX), F32),
+            pltpu.VMEM((tiles, 3, PIX), F32),
         ]
         + [dma(devices)] * 6
         + [dma(3)],
@@ -590,7 +599,7 @@
 
 def pull(here, centres, shape_raw, logit, camera, moving, fixed, owners):
     return pl.pallas_call(
-        partial(pull_kernel, camera.shape[0], here),
+        partial(pull_kernel, camera.shape[2], here),
         out_shape=(
             shape(centres.shape),
             shape(shape_raw.shape),
@@ -619,14 +628,14 @@
         shape_raw,
         logit,
         colours,
-        camera,
-        target.reshape(tiles, 3, PIX),
+        camera.transpose(1, 2, 0),
+        target.transpose(0, 2, 1, 3),
     )
     d_centres, d_shape, d_logit, d_colours, owners = pull(
-        here, centres, shape_raw, logit, camera, moving, fixed, owners
+        here, centres, shape_raw, logit, camera.transpose(1, 2, 0), moving, fixed, owners
     )
     return (
-        image.reshape(target.shape),
+        image.transpose(0, 2, 1, 3),
         d_centres,
         d_shape,
         d_logit.reshape(opacity_logit.shape),

time: 97.1 us -> 92.9 us (0.957)
  Pallas kernels: 93.1 us -> 85.8 us
  local copies, waits for them, and re-layouts: 3.1 us -> 5.93 us
    pallas_call x1, Pallas kernels: 91.6 us -> 84.4 us  [splat(): pl.pallas_call(partial(splat_kernel, sizes, views), out_shape=(shape(targ...]
    unnamed x19, local copies, waits for them, and re-layouts: 3.1 us -> 5.93 us
where the time goes in v5:
time: 92.9 us; the launch traced here: 92.4 us
  Pallas kernels  85.8 us (92%)
  local copies, waits for them, and re-layouts  5.93 us (6%)
    pallas_call x1, Pallas kernels, splat(): pl.pallas_call(partial(splat_kernel, sizes, views), out_shape=(shape(targ...  84.4 us
    unnamed x19, local copies, waits for them, and re-layouts  5.93 us

profile of v5, /device:TPU:1, one launch (start us, length us, event | category | flops | bytes accessed | tf_op | source)
XLA Modules:
  0.0 92.4 jit_solution(5973004429230555921)
XLA Ops:
  0.6 0.0 copy-start.7
  0.6 0.0 copy-start.6
  0.7 0.0 copy-start.8
  0.7 0.7 copy-done.7
  1.3 0.0 copy-done.6
  1.3 0.0 copy-done.8
  1.3 0.0 copy-start
  1.3 0.8 copy-done
  2.1 0.0 copy-start.1
  2.1 0.9 copy-done.1
  3.0 0.0 copy-start.2
  3.0 0.7 copy-done.2
  3.7 0.0 copy-start.3
  3.7 0.8 copy-done.3
  4.5 0.0 copy-start.4
  4.5 0.8 copy-done.4
  5.2 0.0 copy-start.5
  5.2 0.7 copy-done.5
  6.0 84.4 %splat.1 = (f32[2,3,16,256]{3,2,1,0:T(8,128)S(1)}, f32[4,80,128]{2,1,0:T(8,128)S(1)}, f32[32,128]{1,0:T(8,128)S(1)}, s32[2,16]{1,0:T(2,128)S(1)}) custom-call(s32[32,256]{1,0:T(8,128)S(1)} %bitcast.9, s32[32,256]{1,0:T(8,128)S(1)} %bitcast.10, s32[2,16]{1,0:T(2,128)S(1)} %copy-done.8, f32[3,1024]{1,0:T(4,128)S(1)} %copy-done.2, f32[6,1024]{1,0:T(8,128)S(1)} %copy-done, ...), custom_call_target="tpu_custom_call" | custom-call | tf_op jit(solution)/shard_map/splat/pallas_call | solution.py:560
  90.4 1.4 %pull.1 = (f32[3,1024]{1,0:T(4,128)}, f32[6,1024]{1,0:T(8,128)}, f32[8,128]{1,0:T(8,128)}, f32[3,1024]{1,0:T(4,128)}, s32[2,16]{1,0:T(2,128)}) custom-call(f32[3,1024]{1,0:T(4,128)S(1)} %copy-done.2, f32[6,1024]{1,0:T(8,128)S(1)} %copy-done, f32[8,128]{1,0:T(8,128)S(1)} %bitcast.12, f32[2,4,8]{2,1,0:T(4,128)S(1)} %bitcast.14, ...), custom_call_target="tpu_custom_call" | custom-call | tf_op jit(solution)/shard_map/pull/pallas_call | solution.py:601
  91.8 0.6 copy.16
Async XLA Ops:
  0.6 0.7 copy-start.7
  0.6 0.7 copy-start.6
  0.7 0.7 copy-start.8
  1.3 0.8 copy-start
  2.1 0.9 copy-start.1
  3.0 0.7 copy-start.2
  3.7 0.8 copy-start.3
  4.5 0.8 copy-start.4
  5.2 0.7 copy-start.5

commit v6 on v5

--- a/solution.py
+++ b/solution.py
@@ -93,7 +93,7 @@
     ring, views, ids_ref, order_ref, live_ref, centres_ref, shape_ref, logit_ref, colours_ref, camera_ref,
     records_ref, got_ref, owner_ref, rank_ref,
     value_ref, acc_ref, send_ref, answer_ref, recv_ref, moving_ref, fixed_ref,
-    request_send, request_recv, answer_send, answer_recv, local_sem,
+    request_send, request_recv, answer_send, answer_recv, local_sem, loaded,
 ):
     me, devices = ring.me, ring.count
     tiles, slots = ids_ref.shape
@@ -165,6 +165,7 @@
 
     each(1, devices, 16, lambda step: request(ring.after(step)).start())
 
+    loaded()
     centres = [field_of(centres_ref, n) for n in range(3)]
     shape_raw = [field_of(shape_ref, n) for n in range(6)]
     for view in range(views):
@@ -327,11 +328,12 @@
 
 
 def pull_kernel(
-    views, here, centres_ref, shape_ref, logit_ref, camera_ref, moving_ref, fixed_ref, owners_ref,
-    d_centres_ref, d_shape_ref, d_logit_ref, d_colours_ref, next_ref,
+    views, here, centres_ref, shape_ref, logit_ref, camera_ref, moving_ref, fixed_ref, owners_ref, drawn_ref,
+    d_centres_ref, d_shape_ref, d_logit_ref, d_colours_ref, next_ref, image_ref,
 ):
     wide = ROWS * here
     next_ref[...] = owners_ref[...]
+    image_ref[...] = drawn_ref[...]
     centres = [field_of(centres_ref, n) for n in range(3)]
     shape_raw = [field_of(shape_ref, n) for n in range(6)]
     d_centres = [jnp.zeros((ROWS, LANES), F32)] * 3
@@ -502,7 +504,18 @@
 
 
 def splat_kernel(
-    sizes, views, ids_ref, order_ref, live_ref, centres_ref, shape_ref, logit_ref, colours_ref, camera_ref, target_ref,
+    sizes, views, *refs
+):
+    given, rest = refs[:8], refs[8:]
+    held, rest, load_sem = rest[-9:-1], rest[:-9], rest[-1]
+    loads = [pltpu.make_async_copy(a, b, load_sem.at[n]) for n, (a, b) in enumerate(zip(given, held))]
+    for load in loads:
+        load.start()
+    splat(sizes, views, loads, *held, *rest)
+
+
+def splat(
+    sizes, views, loads, ids_ref, order_ref, live_ref, centres_ref, shape_ref, logit_ref, colours_ref, target_ref, camera_ref,
     image_ref, moving_ref, fixed_ref, next_ref,
     records_ref, got_ref, owner_ref, rank_ref, value_ref, ask_acc_ref, send_ref, answer_ref, recv_ref,
     own_moving_ref, own_fixed_ref, cov_ref, odds_ref, high_ref, low_ref, dots_ref, acc_ref, table_ref, given_ref, aims_ref, drawn_ref,
@@ -511,13 +524,20 @@
     ring = Ring(*sizes)
     here, channels, tiles_here, _ = target_ref.shape
     places = [(v, c, t) for v in range(here) for c in range(channels) for t in range(tiles_here)]
-    for v, c, t in places:
-        aims_ref[v * tiles_here + t, c : c + 1, :] = target_ref[v, c, t : t + 1, :]
+
+    def loaded():
+        for load in loads[3:]:
+            load.wait()
+        for v, c, t in places:
+            aims_ref[v * tiles_here + t, c : c + 1, :] = target_ref[v, c, t : t + 1, :]
+
+    for load in loads[:3]:
+        load.wait()
     sent = ask(
         ring, views, ids_ref, order_ref, live_ref, centres_ref, shape_ref, logit_ref, colours_ref, camera_ref,
         records_ref, got_ref, owner_ref, rank_ref,
         value_ref, ask_acc_ref, send_ref, answer_ref, recv_ref, own_moving_ref, own_fixed_ref,
-        request_send, request_recv, answer_send, answer_recv, local_sem,
+        request_send, request_recv, answer_send, answer_recv, local_sem, loaded,
     )
     next_owner(ring, got_ref, live_ref, next_ref)
     render(
@@ -534,11 +554,12 @@
 
 
 VMEM = pl.BlockSpec(memory_space=pltpu.VMEM)
+HBM = pl.BlockSpec(memory_space=pltpu.HBM)
 SMEM = pl.BlockSpec(memory_space=pltpu.SMEM)
 
 
 def params(number=None):
-    limit = 40 * 2**20
+    limit = 60 * 2**20
     if number is None:
         return pltpu.CompilerParams(vmem_limit_bytes=limit)
     return pltpu.CompilerParams(vmem_limit_bytes=limit, collective_id=number, has_side_effects=True)
@@ -552,9 +573,10 @@
     return pltpu.SemaphoreType.DMA(dims)
 
 
-def splat(sizes, ids, order, live, centres, shape_raw, logit, colours, camera, target):
+def splats(sizes, ids, order, live, centres, shape_raw, logit, colours, camera, target):
     tiles, slots = ids.shape
     devices, views, here = sizes[0] * sizes[1], camera.shape[2], live.shape[0]
+    inputs = (ids, order, live, centres, shape_raw, logit, colours, target)
     table = (FIELDS, devices, 1, LANES)
     line = (tiles, 1, slots)
     return pl.pallas_call(
@@ -565,7 +587,7 @@
             shape(((FIELDS - MOVING) * ROWS, LANES)),
             shape(live.shape, I32),
         ),
-        in_specs=[VMEM] * 7 + [SMEM, VMEM],
+        in_specs=[HBM] * 8 + [SMEM],
         out_specs=(VMEM,) * 4,
         scratch_shapes=[
             pltpu.VMEM((FIELDS, devices, LANES), F32),
@@ -591,13 +613,15 @@
             pltpu.VMEM((tiles, 3, PIX), F32),
         ]
         + [dma(devices)] * 6
-        + [dma(3)],
+        + [dma(3)]
+        + [pltpu.VMEM(one.shape, one.dtype) for one in inputs]
+        + [dma(len(inputs))],
         compiler_params=params(0),
         name="splat",
-    )(ids, order, live, centres, shape_raw, logit, colours, camera, target)
-
-
-def pull(here, centres, shape_raw, logit, camera, moving, fixed, owners):
+    )(*inputs, camera)
+
+
+def pull(here, centres, shape_raw, logit, camera, moving, fixed, owners, image):
     return pl.pallas_call(
         partial(pull_kernel, camera.shape[2], here),
         out_shape=(
@@ -606,12 +630,13 @@
             shape(logit.shape),
             shape(centres.shape),
             shape(owners.shape, I32),
+            shape(image.shape),
         ),
-        in_specs=[VMEM] * 3 + [SMEM] + [VMEM] * 3,
-        out_specs=(VMEM,) * 5,
+        in_specs=[VMEM] * 3 + [SMEM] + [VMEM] * 4,
+        out_specs=(VMEM,) * 6,
         compiler_params=params(),
         name="pull",
-    )(centres, shape_raw, logit, camera, moving, fixed, owners)
+    )(centres, shape_raw, logit, camera, moving, fixed, owners, image)
 
 
 def shards(centres, shape_raw, opacity_logit, colours, camera, target, intersection_ids, depth_order, live_count):
@@ -619,7 +644,7 @@
     here, tiles_here, slots = intersection_ids.shape
     tiles = here * tiles_here
     logit = opacity_logit.reshape(ROWS, LANES)
-    image, moving, fixed, owners = splat(
+    image, moving, fixed, owners = splats(
         sizes,
         intersection_ids.reshape(tiles, slots),
         depth_order.reshape(tiles, slots),
@@ -631,8 +656,8 @@
         camera.transpose(1, 2, 0),
         target.transpose(0, 2, 1, 3),
     )
-    d_centres, d_shape, d_logit, d_colours, owners = pull(
-        here, centres, shape_raw, logit, camera.transpose(1, 2, 0), moving, fixed, owners
+    d_centres, d_shape, d_logit, d_colours, owners, image = pull(
+        here, centres, shape_raw, logit, camera.transpose(1, 2, 0), moving, fixed, owners, image
     )
     return (
         image.transpose(0, 2, 1, 3),

time: 92.9 us -> 88.8 us (0.956)
  local copies, waits for them, and re-layouts: 5.93 us -> 0 us
  Pallas kernels: 85.8 us -> 87.9 us
    unnamed x19 -> x0, local copies, waits for them, and re-layouts: 5.93 us -> none
    pallas_call x1, Pallas kernels: 84.4 us -> 86.1 us  [splats(): pl.pallas_call(partial(splat_kernel, sizes, views), out_shape=(shape(targ...]
where the time goes in v6:
time: 88.8 us; the launch traced here: 88.6 us
  Pallas kernels  87.9 us (99%)
    pallas_call x1, Pallas kernels, splats(): pl.pallas_call(partial(splat_kernel, sizes, views), out_shape=(shape(targ...  86.1 us
    pallas_call x1, Pallas kernels, pull(): pl.pallas_call(partial(pull_kernel, camera.shape[2], here), out_shape=(sh...  1.85 us

profile of v6, /device:TPU:1, one launch (start us, length us, event | category | flops | bytes accessed | tf_op | source)
XLA Modules:
  0.0 88.6 jit_solution(12869711888987100295)
XLA Ops:
  0.6 86.1 %splat.1 = (f32[2,3,16,256]{3,2,1,0:T(8,128)}, f32[4,80,128]{2,1,0:T(8,128)}, f32[32,128]{1,0:T(8,128)}, s32[2,16]{1,0:T(2,128)}) custom-call(s32[32,256]{1,0:T(8,128)} %bitcast.8, s32[32,256]{1,0:T(8,128)} %bitcast.9, s32[2,16]{1,0:T(2,128)} %refs_2_.1, f32[3,1024]{1,0:T(4,128)} %centres_ref.1, f32[6,1024]{1,0:T(8,128)} %shape_ref.1, f32[8,128]{1,0:T(8,128)} %bitcast.10, ...), custom_call_target="tpu_custom_call" | custom-call | tf_op jit(solution)/shard_map/splat/pallas_call | solution.py:582
  86.7 1.8 %pull.1 = (f32[3,1024]{1,0:T(4,128)}, f32[6,1024]{1,0:T(8,128)}, f32[8,128]{1,0:T(8,128)}, f32[3,1024]{1,0:T(4,128)}, s32[2,16]{1,0:T(2,128)}, /*index=5*/f32[2,3,16,256]{3,2,1,0:T(8,128)}) custom-call(f32[3,1024]{1,0:T(4,128)} %centres_ref.1, f32[6,1024]{1,0:T(8,128)} %shape_ref.1, f32[8,128]{1,0:T(8,128)} %bitcast.11, f32[2,4,8]{2,1,0:T(4,128)} %bitcast.13, ...), custom_call_target="tpu_custom_call" | custom-call | tf_op jit(solution)/shard_map/pull/pallas_call | solution.py:625

commit v7 on v6

--- a/solution.py
+++ b/solution.py
@@ -14,7 +14,7 @@
 ROWS = 8
 FIELDS = 9
 MOVING = 5
-TOGETHER = 4
+TOGETHER = 8
 F32 = jnp.float32
 BF16 = jnp.bfloat16
 I32 = jnp.int32

time: 88.8 us -> 87.8 us (0.989)
  Pallas kernels: 87.9 us -> 86.9 us
    pallas_call x1, Pallas kernels: 86.1 us -> 85.1 us  [splats(): pl.pallas_call(partial(splat_kernel, sizes, views), out_shape=(shape(targ...]
where the time goes in v7:
time: 87.8 us; the launch traced here: 87.6 us
  Pallas kernels  86.9 us (99%)
    pallas_call x1, Pallas kernels, splats(): pl.pallas_call(partial(splat_kernel, sizes, views), out_shape=(shape(targ...  85.1 us
    pallas_call x1, Pallas kernels, pull(): pl.pallas_call(partial(pull_kernel, camera.shape[2], here), out_shape=(sh...  1.85 us

profile of v7, /device:TPU:1, one launch (start us, length us, event | category | flops | bytes accessed | tf_op | source)
XLA Modules:
  0.0 87.6 jit_solution(12450763301605511819)
XLA Ops:
  0.6 85.1 %splat.1 = (f32[2,3,16,256]{3,2,1,0:T(8,128)}, f32[4,80,128]{2,1,0:T(8,128)}, f32[32,128]{1,0:T(8,128)}, s32[2,16]{1,0:T(2,128)}) custom-call(s32[32,256]{1,0:T(8,128)} %bitcast.8, s32[32,256]{1,0:T(8,128)} %bitcast.9, s32[2,16]{1,0:T(2,128)} %refs_2_.1, f32[3,1024]{1,0:T(4,128)} %centres_ref.1, f32[6,1024]{1,0:T(8,128)} %shape_ref.1, f32[8,128]{1,0:T(8,128)} %bitcast.10, ...), custom_call_target="tpu_custom_call" | custom-call | tf_op jit(solution)/shard_map/splat/pallas_call | solution.py:582
  85.7 1.8 %pull.1 = (f32[3,1024]{1,0:T(4,128)}, f32[6,1024]{1,0:T(8,128)}, f32[8,128]{1,0:T(8,128)}, f32[3,1024]{1,0:T(4,128)}, s32[2,16]{1,0:T(2,128)}, /*index=5*/f32[2,3,16,256]{3,2,1,0:T(8,128)}) custom-call(f32[3,1024]{1,0:T(4,128)} %centres_ref.1, f32[6,1024]{1,0:T(8,128)} %shape_ref.1, f32[8,128]{1,0:T(8,128)} %bitcast.11, f32[2,4,8]{2,1,0:T(4,128)} %bitcast.13, ...), custom_call_target="tpu_custom_call" | custom-call | tf_op jit(solution)/shard_map/pull/pallas_call | solution.py:625

commit v8 on v7

--- a/solution.py
+++ b/solution.py
@@ -125,13 +125,14 @@
     def tile(t, before):
         owner, value = owner_ref[t], value_ref[t]
         named = peers == owner
-        count = dot_nn(named.astype(BF16), upto)
+        flags = named.astype(BF16)
+        count = dot_nn(flags, upto)
         rank = jnp.sum(jnp.where(named, count + before, 0.0), axis=0, keepdims=True) - 1.0
         rank = rank.astype(I32)
         rank_ref[t] = rank
         at_rank = (ranks == rank).astype(BF16)
         parts = [(value & 255).astype(F32), (value >> 8).astype(F32)]
-        left = jnp.concatenate([jnp.where(named, part, 0.0).astype(BF16) for part in parts], axis=0)
+        left = jnp.concatenate([flags * part.astype(BF16) for part in parts], axis=0)
         acc_ref[...] += dot_nt(left, at_rank)
         return before + count[:, slots - 1 :]
 

time: 87.8 us -> 87.8 us (level)
  no operation moved by 1% of the time
where the time goes in v8:
time: 87.8 us; the launch traced here: 87.6 us
  Pallas kernels  86.9 us (99%)
    pallas_call x1, Pallas kernels, splats(): pl.pallas_call(partial(splat_kernel, sizes, views), out_shape=(shape(targ...  85.1 us
    pallas_call x1, Pallas kernels, pull(): pl.pallas_call(partial(pull_kernel, camera.shape[2], here), out_shape=(sh...  1.85 us

profile of v8, /device:TPU:1, one launch (start us, length us, event | category | flops | bytes accessed | tf_op | source)
XLA Modules:
  0.0 87.6 jit_solution(11476827051741640810)
XLA Ops:
  0.6 85.1 %splat.1 = (f32[2,3,16,256]{3,2,1,0:T(8,128)}, f32[4,80,128]{2,1,0:T(8,128)}, f32[32,128]{1,0:T(8,128)}, s32[2,16]{1,0:T(2,128)}) custom-call(s32[32,256]{1,0:T(8,128)} %bitcast.8, s32[32,256]{1,0:T(8,128)} %bitcast.9, s32[2,16]{1,0:T(2,128)} %refs_2_.1, f32[3,1024]{1,0:T(4,128)} %centres_ref.1, f32[6,1024]{1,0:T(8,128)} %shape_ref.1, f32[8,128]{1,0:T(8,128)} %bitcast.10, ...), custom_call_target="tpu_custom_call" | custom-call | tf_op jit(solution)/shard_map/splat/pallas_call | solution.py:583
  85.7 1.8 %pull.1 = (f32[3,1024]{1,0:T(4,128)}, f32[6,1024]{1,0:T(8,128)}, f32[8,128]{1,0:T(8,128)}, f32[3,1024]{1,0:T(4,128)}, s32[2,16]{1,0:T(2,128)}, /*index=5*/f32[2,3,16,256]{3,2,1,0:T(8,128)}) custom-call(f32[3,1024]{1,0:T(4,128)} %centres_ref.1, f32[6,1024]{1,0:T(8,128)} %shape_ref.1, f32[8,128]{1,0:T(8,128)} %bitcast.11, f32[2,4,8]{2,1,0:T(4,128)} %bitcast.13, ...), custom_call_target="tpu_custom_call" | custom-call | tf_op jit(solution)/shard_map/pull/pallas_call | solution.py:626
